TPU v7x, 256 devices: a whole 4x4x8 slice. The times are simulated.
256 devices in a mesh: pipe: 4 (over z_lo), dp: 2 (over z_hi), expert: 32 (over y, x, core).
Axes of the slice: x: 4, y: 4, z: 8 (z_hi: 2, z_lo: 4; z = z_hi * 4 + z_lo), core: 2. Of those that a mesh axis runs over, the one named last changes fastest.
Arguments:
- x_fwd: bfloat16 [4, 4096, 3584], P('pipe', ('dp', 'expert')), may hold values from -6 to 6
- routes_fwd: int32 [4, 4096, 2], P('pipe', ('dp', 'expert')), may hold values from 0 to 31, all different within a row; in each aligned block of 64 rows (0 to 63, 64 to 127, ..., all dimensions but the last counted through in order) at most 6 rows name the same one
- x_bwd: bfloat16 [4, 4096, 3584], P('pipe', ('dp', 'expert')), may hold values from -6 to 6
- cot_bwd: bfloat16 [4, 4096, 3584], P('pipe', ('dp', 'expert')), may hold values from -6 to 6
- routes_bwd: int32 [4, 4096, 2], P('pipe', ('dp', 'expert')), may hold values from 0 to 31, all different within a row; in each aligned block of 64 rows (0 to 63, 64 to 127, ..., all dimensions but the last counted through in order) at most 6 rows name the same one
- router_weight: bfloat16 [4, 3584, 32], P('pipe'), may hold values from -0.09375 to 0.09375
- gate_weight: bfloat16 [4, 32, 3584, 1024], P('pipe', 'expert', None, 'dp'), may hold values from -0.09375 to 0.09375
- up_weight: bfloat16 [4, 32, 3584, 1024], P('pipe', 'expert', None, 'dp'), may hold values from -0.09375 to 0.09375
- down_weight: bfloat16 [4, 32, 1024, 3584], P('pipe', 'expert', 'dp'), may hold values from -0.1875 to 0.1875
- attn_input: bfloat16 [4, 4096, 3584], P('pipe', ('dp', 'expert')), may hold values from -16 to 16
- latent_cot: bfloat16 [4, 4096, 512], P('pipe', ('dp', 'expert')), may hold values from -0.09375 to 0.09375
Outputs:
- fwd_sent: bfloat16 [4, 4096, 3584], P('pipe', ('dp', 'expert'))
- bwd_sent: bfloat16 [4, 4096, 3584], P('pipe', ('dp', 'expert'))
- kv_grad: float32 [4, 3584, 512], P('pipe', ('dp', 'expert'))
Inputs may be any that keep to these rules, and one draw needn't show every extreme that they name: `routes_fwd`: A token names 2 different experts; in each block of 64 consecutive tokens of a section no expert is named by more than 6 routes, a bound that some block reaches. `routes_bwd`: A token names 2 different experts; in each block of 64 consecutive tokens of a section no expert is named by more than 6 routes, a bound that some block reaches.
All inputs are finite; a program needn't handle non-finite values.
Results may differ from a plain program's by a relative error of at most 0.0054.
Values may be sent and summed in bfloat16 or wider, within the bound.
A program may use at most 128 MiB of HBM per device.

v0:
```python
import jax
import jax.numpy as jnp
from jax import lax
from jax.sharding import PartitionSpec as P

TOP = 2


ROUTE_SCALE = 2.5


def shifted(array, axis, by):
    peers = lax.axis_size(axis)
    return lax.ppermute(array, axis, [(i, (i + by) % peers) for i in range(peers)])


def slot_keys(routes, count_experts, capacity):
    route_count = routes.shape[0] * routes.shape[1]
    flat_routes = routes.reshape(route_count)
    expert_ids = jnp.arange(count_experts, dtype=jnp.int32)
    member = (flat_routes[:, None] == expert_ids[None, :]).astype(jnp.int32)
    earlier = jnp.cumsum(member, axis=0) - member
    slot_index = jnp.sum(earlier * member, axis=1)
    return (flat_routes * capacity + slot_index).reshape(routes.shape)


def place_rows(slot_key, tokens, positions):
    targets = jnp.arange(positions, dtype=jnp.int32)
    member = jnp.sum((slot_key[None, :, :] == targets[:, None, None]).astype(jnp.float32), axis=2)
    placed = jnp.dot(member.astype(jnp.bfloat16), tokens, preferred_element_type=jnp.float32)
    return placed.astype(jnp.bfloat16)


def route_gates(tokens, router, routes):
    logits = jnp.dot(tokens, router, preferred_element_type=jnp.float32)
    expert_ids = jnp.arange(router.shape[1], dtype=jnp.int32)
    route_table = (routes[:, :, None] == expert_ids[None, None, :]).astype(jnp.float32)
    chosen = jnp.sum(logits[:, None, :] * route_table, axis=2)
    route_rates = jax.nn.sigmoid(chosen)
    rate_total = jnp.sum(route_rates, axis=1, keepdims=True)
    return (ROUTE_SCALE * route_rates / rate_total, route_rates, rate_total, route_table)


def expert_forward(row_block, gate_matrix, up_matrix, down_matrix):
    gate_act = jnp.dot(row_block, gate_matrix, preferred_element_type=jnp.float32)
    up_act = jnp.dot(row_block, up_matrix, preferred_element_type=jnp.float32)
    hidden = (gate_act * jax.nn.sigmoid(gate_act) * up_act).astype(jnp.bfloat16)
    return jnp.dot(hidden, down_matrix, preferred_element_type=jnp.float32)


def expert_backward(row_block, cotangent, gate_matrix, up_matrix, down_matrix):
    gate_act = jnp.dot(row_block, gate_matrix, preferred_element_type=jnp.float32)
    up_act = jnp.dot(row_block, up_matrix, preferred_element_type=jnp.float32)
    sigmoid_gate = jax.nn.sigmoid(gate_act)
    active = gate_act * sigmoid_gate
    hidden = (active * up_act).astype(jnp.bfloat16)
    full_out = jnp.dot(hidden, down_matrix, preferred_element_type=jnp.float32)
    inner_dot = jnp.sum(cotangent.astype(jnp.float32) * full_out, axis=1)
    contract = (((1,), (1,)), ((), ()))
    grad_hidden = lax.dot_general(
        cotangent, down_matrix, contract, preferred_element_type=jnp.float32
    )
    grad_gate = (
        grad_hidden * up_act * sigmoid_gate * (1.0 + gate_act * (1.0 - sigmoid_gate))
    ).astype(jnp.bfloat16)
    grad_up = (grad_hidden * active).astype(jnp.bfloat16)
    back_rows = lax.dot_general(
        grad_gate, gate_matrix, contract, preferred_element_type=jnp.float32
    )
    back_rows = back_rows + lax.dot_general(
        grad_up, up_matrix, contract, preferred_element_type=jnp.float32
    )
    return (back_rows, inner_dot)


def combine_rows(gates, slot_key, returned):
    picked = jnp.take(returned, slot_key.reshape(-1), axis=0)
    picked = picked.reshape(slot_key.shape + (returned.shape[1],))
    return jnp.sum(gates[:, :, None] * picked.astype(jnp.float32), axis=1)


def router_grad(route_rates, rate_total, route_table, inner_picked):
    weighted = jnp.sum(inner_picked * route_rates, axis=1, keepdims=True)
    grad_rates = ROUTE_SCALE * (inner_picked / rate_total - weighted / (rate_total * rate_total))
    grad_logit = grad_rates * route_rates * (1.0 - route_rates)
    return jnp.sum(grad_logit[:, :, None] * route_table, axis=1).astype(jnp.bfloat16)


def body(
    x_fwd,
    routes_fwd,
    x_bwd,
    cot_bwd,
    routes_bwd,
    router_weight,
    gate_weight,
    up_weight,
    down_weight,
    attn_input,
    latent_cot,
):
    count_experts = lax.axis_size("expert")
    tokens_fwd = x_fwd[0]
    tokens_bwd = x_bwd[0]
    cotangent = cot_bwd[0]
    router = router_weight[0]
    model_width = tokens_fwd.shape[1]
    capacity = 3 * tokens_fwd.shape[0] * TOP // (2 * count_experts)
    positions = count_experts * capacity
    block_shape = (count_experts, capacity, model_width)
    keys_fwd = slot_keys(routes_fwd[0], count_experts, capacity)
    keys_bwd = slot_keys(routes_bwd[0], count_experts, capacity)
    sent_fwd = place_rows(keys_fwd, tokens_fwd, positions).reshape(block_shape)
    sent_x = place_rows(keys_bwd, tokens_bwd, positions).reshape(block_shape)
    sent_g = place_rows(keys_bwd, cotangent, positions).reshape(block_shape)
    came_fwd, came_x, came_g = (
        lax.all_to_all(sent_fwd, "expert", split_axis=0, concat_axis=0, tiled=True),
        lax.all_to_all(sent_x, "expert", split_axis=0, concat_axis=0, tiled=True),
        lax.all_to_all(sent_g, "expert", split_axis=0, concat_axis=0, tiled=True),
    )
    gate_part = gate_weight[0, 0]
    up_part = up_weight[0, 0]
    down_part = down_weight[0, 0]
    gate_full, up_full, down_full = (
        lax.all_gather(gate_part, "dp", axis=1, tiled=True),
        lax.all_gather(up_part, "dp", axis=1, tiled=True),
        lax.all_gather(down_part, "dp", axis=0, tiled=True),
    )
    out_fwd = expert_forward(
        came_fwd.reshape(positions, model_width), gate_full, up_full, down_full
    )
    back_rows, inner_dot = expert_backward(
        came_x.reshape(positions, model_width),
        came_g.reshape(positions, model_width),
        gate_full,
        up_full,
        down_full,
    )
    ret_fwd = out_fwd.astype(jnp.bfloat16).reshape(block_shape)
    ret_back = back_rows.astype(jnp.bfloat16).reshape(block_shape)
    ret_inner = inner_dot.astype(jnp.bfloat16).reshape(count_experts, capacity)
    got_fwd, got_back, got_inner = (
        lax.all_to_all(ret_fwd, "expert", split_axis=0, concat_axis=0, tiled=True),
        lax.all_to_all(ret_back, "expert", split_axis=0, concat_axis=0, tiled=True),
        lax.all_to_all(ret_inner, "expert", split_axis=0, concat_axis=0, tiled=True),
    )
    gates_fwd = route_gates(tokens_fwd, router, routes_fwd[0])[0]
    y_fwd = tokens_fwd.astype(jnp.float32) + combine_rows(
        gates_fwd, keys_fwd, got_fwd.reshape(positions, model_width)
    )
    y_fwd = y_fwd.astype(jnp.bfloat16)
    gates_bwd, route_rates, rate_total, route_table = route_gates(tokens_bwd, router, routes_bwd[0])
    inner_picked = jnp.take(got_inner.reshape(positions), keys_bwd.reshape(-1), axis=0)
    inner_picked = inner_picked.reshape(keys_bwd.shape).astype(jnp.float32)
    grad_logits = router_grad(route_rates, rate_total, route_table, inner_picked)
    router_back = lax.dot_general(
        grad_logits, router, (((1,), (1,)), ((), ())), preferred_element_type=jnp.float32
    )
    dx_bwd = cotangent.astype(jnp.float32) + combine_rows(
        gates_bwd, keys_bwd, got_back.reshape(positions, model_width)
    )
    dx_bwd = (dx_bwd + router_back).astype(jnp.bfloat16)
    sent_next = shifted(jnp.stack([y_fwd[None], dx_bwd[None]]), "pipe", 1)
    attn_local = attn_input[0]
    latent_local = latent_cot[0]
    kv_part = lax.psum_scatter(
        lax.dot_general(
            attn_local, latent_local, (((0,), (0,)), ((), ())), preferred_element_type=jnp.float32
        ),
        ("dp", "expert"),
        scatter_dimension=0,
        tiled=True,
    )
    return (sent_next[0], sent_next[1], kv_part[None])


def solution(mesh):
    in_specs = (
        P("pipe", ("dp", "expert"), None),
        P("pipe", ("dp", "expert"), None),
        P("pipe", ("dp", "expert"), None),
        P("pipe", ("dp", "expert"), None),
        P("pipe", ("dp", "expert"), None),
        P("pipe", None, None),
        P("pipe", "expert", None, "dp"),
        P("pipe", "expert", None, "dp"),
        P("pipe", "expert", "dp", None),
        P("pipe", ("dp", "expert"), None),
        P("pipe", ("dp", "expert"), None),
    )
    out_specs = (
        P("pipe", ("dp", "expert"), None),
        P("pipe", ("dp", "expert"), None),
        P("pipe", ("dp", "expert"), None),
    )
    return jax.shard_map(body, mesh=mesh, in_specs=in_specs, out_specs=out_specs, check_vma=False)
```

profile of v0, /device:TPU:32, one launch (start us, length us, event | category | flops | bytes accessed | tf_op | source)
XLA Modules:
  0.0 931.7 jit_solution(17590736246160245553)
XLA Ops:
  11.8 1.5 reshape.252
  13.4 7.4 all-to-all-start.3
  20.8 1.6 convolution_convert_fusion.1
  22.4 3.4 reshape.250
  25.8 21.9 %all-to-all-done.3 = bf16[32,6,3584]{2,1,0:T(8,128)(2,1)S(1)} async-done(((bf16[32,6,3584]{2,1,0:T(8,128)(2,1)}), bf16[32,6,3584]{2,1,0:T(8,128)(2,1)S(1)}, u32[]{:S(2)}, u32[]{:S(2)}) %all-to-all-start.3) | async-done | bytes 1376288 | tf_op jit(solution)/shard_map/all_to_all | solution.py:118
  47.7 4.7 all-to-all-start.2
  52.5 4.1 fusion.45
  58.8 1.6 convolution_convert_fusion.2
  60.5 3.4 reshape.246
  63.9 15.8 %all-to-all-done.2 = bf16[32,6,3584]{2,1,0:T(8,128)(2,1)} async-done(((bf16[32,6,3584]{2,1,0:T(8,128)(2,1)}), bf16[32,6,3584]{2,1,0:T(8,128)(2,1)}, u32[]{:S(2)}, u32[]{:S(2)}) %all-to-all-start.2) | async-done | bytes 1376288 | tf_op jit(solution)/shard_map/all_to_all | solution.py:119
  79.7 4.7 all-to-all-start
  85.0 1.4 reshape.253
  86.4 2.4 reshape.251
  88.8 21.9 %all-to-all-done = bf16[32,6,3584]{2,1,0:T(8,128)(2,1)} async-done(((bf16[32,6,3584]{2,1,0:T(8,128)(2,1)}), bf16[32,6,3584]{2,1,0:T(8,128)(2,1)}, u32[]{:S(2)}, u32[]{:S(2)}) %all-to-all-start) | async-done | bytes 1376288 | tf_op jit(solution)/shard_map/all_to_all | solution.py:117
  110.8 2.4 reshape.247
  113.2 80.1 %all-gather.7.cloned.1.call-done = bf16[1,1,3584,1024]{3,2,1,0:T(8,128)(2,1)} async-done(((bf16[1,1,3584,512]{3,2,1,0:T(8,128)(2,1)}), bf16[1,1,3584,1024]{3,2,1,0:T(8,128)(2,1)}) %all-gather.7.cloned.1.call-update) | async-done | bytes 7340048 | tf_op jit(solution)/shard_map/all_gather | solution.py:125
  193.3 6.0 fusion.14
  199.3 151.9 %all-gather.9.cloned.1.call-done = bf16[1,1,3584,1024]{3,2,1,0:T(8,128)(2,1)} async-done(((bf16[1,1,3584,512]{3,2,1,0:T(8,128)(2,1)}), bf16[1,1,3584,1024]{3,2,1,0:T(8,128)(2,1)}) %all-gather.9.cloned.1.call-update) | async-done | bytes 7340048 | tf_op jit(solution)/shard_map/all_gather | solution.py:126
  351.2 6.0 fusion.8
  357.2 163.2 %all-gather.11.cloned.1.call-done = bf16[1,1,1024,3584]{3,2,1,0:T(8,128)(2,1)} async-done(((bf16[1,1,512,3584]{3,2,1,0:T(8,128)(2,1)}), bf16[1,1,1024,3584]{3,2,1,0:T(8,128)(2,1)}) %all-gather.11.cloned.1.call-update) | async-done | bytes 7340048 | tf_op jit(solution)/shard_map/all_gather | solution.py:127
  520.4 5.3 fusion.32
  525.7 0.7 convert_element_type.149
  526.5 39.0 %all-to-all-start.5 = ((bf16[32,1,6]{2,1,0:T(2,128)(2,1)}), bf16[32,1,6]{2,1,0:T(2,128)(2,1)S(1)}, u32[]{:S(2)}, u32[]{:S(2)}) async-start(bf16[32,1,6]{2,1,0:T(2,128)(2,1)} %convert_element_type.149), calls=%async_computation.5 | async-start | bytes 32768 | tf_op jit(solution)/shard_map/all_to_all | solution.py:145
  565.5 5.6 fusion.16
  571.0 9.7 %fusion.27 = bf16[192,3584]{1,0:T(8,128)(2,1)} fusion(bf16[1,1,1024,3584]{3,2,1,0:T(8,128)(2,1)} %all-gather.11.cloned.1.call-done, bf16[192,3584]{1,0:T(8,128)(2,1)S(1)} %reshape.247, bf16[1,1,3584,1024]{3,2,1,0:T(8,128)(2,1)} %all-gather.9.cloned.1.call-done, f32[192,1024]{1,0:T(8,128)} %fusion.16), kind=kOutput, calls=%fused_computation.24 | convolution fusion | flops 2820440064 | bytes 18219008 | tf_op jit(solution)/shard_map/dot_general | solution.py:48
  580.7 6.6 fusion.2
  587.3 1.5 reshape.248
  588.9 7.3 all-to-all-start.1
  596.2 6.1 fusion.6
  602.4 5.7 fusion.24
  608.1 1.6 reshape.254
  609.8 1.2 gather_fusion
  611.4 12.8 %all-to-all-done.1 = bf16[32,6,3584]{2,1,0:T(8,128)(2,1)S(1)} async-done(((bf16[32,6,3584]{2,1,0:T(8,128)(2,1)}), bf16[32,6,3584]{2,1,0:T(8,128)(2,1)S(1)}, u32[]{:S(2)}, u32[]{:S(2)}) %all-to-all-start.1) | async-done | bytes 1376288 | tf_op jit(solution)/shard_map/all_to_all | solution.py:143
  624.2 4.9 all-to-all-start.4
  629.9 1.1 gather_fusion.1
  631.0 1.4 select_convert_fusion.1
  632.5 2.4 reshape.258
  634.9 22.4 %all-to-all-done.4 = bf16[32,6,3584]{2,1,0:T(8,128)(2,1)} async-done(((bf16[32,6,3584]{2,1,0:T(8,128)(2,1)}), bf16[32,6,3584]{2,1,0:T(8,128)(2,1)}, u32[]{:S(2)}, u32[]{:S(2)}) %all-to-all-start.4) | async-done | bytes 1376288 | tf_op jit(solution)/shard_map/all_to_all | solution.py:144
  657.3 2.4 reshape.255
  659.7 2.0 gather_fusion.2
  661.8 2.7 select_convert_fusion
  664.5 3.3 reshape.259
  667.8 4.1 multiply_reduce_fusion
  672.3 2.5 multiply_reduce_fusion.1
  675.0 0.8 collective-permute-start
  675.8 27.5 %collective-permute-done = bf16[2,1,64,3584]{3,2,1,0:T(8,128)(2,1)S(1)} collective-permute-done((bf16[2,1,64,3584]{3,2,1,0:T(8,128)(2,1)S(1)}, bf16[2,1,64,3584]{3,2,1,0:T(8,128)(2,1)S(1)}, u32[]{:S(2)}, u32[]{:S(2)}) %collective-permute-start) | collective-permute-done | bytes 917536 | tf_op jit(solution)/shard_map/ppermute | solution.py:14
  703.3 1.0 slice_bitcast_fusion
  704.2 220.3 %reduce-scatter.2.cloned.1.call-done = f32[56,512]{1,0:T(8,128)} async-done(((f32[3584,512]{1,0:T(8,128)}), f32[56,512]{1,0:T(8,128)}) %reduce-scatter.2.cloned.1.call-update) | async-done | bytes 114704 | tf_op jit(solution)/shard_map/reduce_scatter | solution.py:166
  (89 shorter events, 8.2 us)
Async XLA Ops:
  8.0 44.5 %copy-start = (bf16[1,64,3584]{2,1,0:T(8,128)(2,1)S(1)}, bf16[1,64,3584]{2,1,0:T(8,128)(2,1)}, u32[]{:S(2)}) copy-start(bf16[1,64,3584]{2,1,0:T(8,128)(2,1)} %param.22) | copy-start | bytes 1376260
  8.0 185.3 %all-gather.7.cloned.1.call-start = ((), (), s32[]{:S(2)}) async-start(), calls=%async_computation.8 | async-start | bytes 11010048 | tf_op jit(solution)/shard_map/all_gather | solution.py:125
  8.7 342.5 %all-gather.9.cloned.1.call-start = ((), (), s32[]{:S(2)}) async-start(), calls=%async_computation.9 | async-start | bytes 11010048 | tf_op jit(solution)/shard_map/all_gather | solution.py:126
  9.5 0.8 copy-start.14
  9.5 1.8 copy-start.5
  9.5 510.9 %all-gather.11.cloned.1.call-start = ((), (), s32[]{:S(2)}) async-start(), calls=%async_computation.10 | async-start | bytes 11010048 | tf_op jit(solution)/shard_map/all_gather | solution.py:127
  13.3 7.5 copy-start.6
  13.4 34.4 %all-to-all-start.3 = ((bf16[32,6,3584]{2,1,0:T(8,128)(2,1)}), bf16[32,6,3584]{2,1,0:T(8,128)(2,1)S(1)}, u32[]{:S(2)}, u32[]{:S(2)}) async-start(bf16[32,6,3584]{2,1,0:T(8,128)(2,1)} %reshape.252), calls=%async_computation.3 | async-start | bytes 3670016 | tf_op jit(solution)/shard_map/all_to_all | solution.py:118
  25.8 26.7 %copy-start.13 = (bf16[1,64,512]{2,1,0:T(8,128)(2,1)S(1)}, bf16[1,64,512]{2,1,0:T(8,128)(2,1)}, u32[]{:S(2)}) copy-start(bf16[1,64,512]{2,1,0:T(8,128)(2,1)} %param.23) | copy-start | bytes 196612
  47.7 32.0 %all-to-all-start.2 = ((bf16[32,6,3584]{2,1,0:T(8,128)(2,1)}), bf16[32,6,3584]{2,1,0:T(8,128)(2,1)}, u32[]{:S(2)}, u32[]{:S(2)}) async-start(bf16[32,6,3584]{2,1,0:T(8,128)(2,1)} %reshape.250), calls=%async_computation.2 | async-start | bytes 3670016 | tf_op jit(solution)/shard_map/all_to_all | solution.py:119
  52.5 872.1 %reduce-scatter.2.cloned.1.call-start = ((), (), s32[]{:S(2)}) async-start(), calls=%async_computation.7 | async-start | bytes 7454720 | tf_op jit(solution)/shard_map/reduce_scatter | solution.py:166
  56.7 0.7 copy-start.15
  56.7 2.2 copy-start.2
  63.8 20.7 %copy-start.4 = (bf16[1,3584,32]{1,2,0:T(8,128)(2,1)S(1)}, bf16[1,3584,32]{1,2,0:T(8,128)(2,1)}, u32[]{:S(2)}) copy-start(bf16[1,3584,32]{1,2,0:T(8,128)(2,1)} %param.18) | copy-start | bytes 688132
  79.7 31.1 %all-to-all-start = ((bf16[32,6,3584]{2,1,0:T(8,128)(2,1)}), bf16[32,6,3584]{2,1,0:T(8,128)(2,1)}, u32[]{:S(2)}, u32[]{:S(2)}) async-start(bf16[32,6,3584]{2,1,0:T(8,128)(2,1)} %reshape.246), calls=%async_computation | async-start | bytes 3670016 | tf_op jit(solution)/shard_map/all_to_all | solution.py:117
  526.5 62.4 %all-to-all-start.5 = ((bf16[32,1,6]{2,1,0:T(2,128)(2,1)}), bf16[32,1,6]{2,1,0:T(2,128)(2,1)S(1)}, u32[]{:S(2)}, u32[]{:S(2)}) async-start(bf16[32,1,6]{2,1,0:T(2,128)(2,1)} %convert_element_type.149), calls=%async_computation.5 | async-start | bytes 32768 | tf_op jit(solution)/shard_map/all_to_all | solution.py:145
  580.7 6.6 copy-start.8
  588.9 7.3 copy-start.9
  588.9 35.4 %all-to-all-start.1 = ((bf16[32,6,3584]{2,1,0:T(8,128)(2,1)}), bf16[32,6,3584]{2,1,0:T(8,128)(2,1)S(1)}, u32[]{:S(2)}, u32[]{:S(2)}) async-start(bf16[32,6,3584]{2,1,0:T(8,128)(2,1)} %reshape.248), calls=%async_computation.1 | async-start | bytes 3670016 | tf_op jit(solution)/shard_map/all_to_all | solution.py:143
  596.2 6.1 copy-start.10
  596.2 6.1 copy-start.11
  596.2 6.1 copy-start.12
  624.2 33.1 %all-to-all-start.4 = ((bf16[32,6,3584]{2,1,0:T(8,128)(2,1)}), bf16[32,6,3584]{2,1,0:T(8,128)(2,1)}, u32[]{:S(2)}, u32[]{:S(2)}) async-start(bf16[32,6,3584]{2,1,0:T(8,128)(2,1)} %reshape.254), calls=%async_computation.4 | async-start | bytes 3670016 | tf_op jit(solution)/shard_map/all_to_all | solution.py:144
  667.8 4.1 copy-start.7
  672.2 2.5 copy-start.3
  674.8 249.8 %copy-start.1 = (bf16[1,64,3584]{2,1,0:T(8,128)(2,1)S(1)}, bf16[1,64,3584]{2,1,0:T(8,128)(2,1)}, u32[]{:S(2)}) copy-start(bf16[1,64,3584]{2,1,0:T(8,128)(2,1)} %param.22) | copy-start | bytes 1376260
  675.0 28.3 %collective-permute-start = (bf16[2,1,64,3584]{3,2,1,0:T(8,128)(2,1)S(1)}, bf16[2,1,64,3584]{3,2,1,0:T(8,128)(2,1)S(1)}, u32[]{:S(2)}, u32[]{:S(2)}) collective-permute-start(bf16[2,1,64,3584]{3,2,1,0:T(8,128)(2,1)S(1)} %pad_maximum_fusion), channel_id=1, source_target_pairs={{0,64},{64,128},{128,192},{192,0},{1,65},{65,129},{129,193},{193,1... | collective-permute-start | bytes 2752520 | tf_op jit(solution)/shard_map/ppermute | solution.py:14
Sparse Core Ops, SparseCore 0:
  10.6 182.5 all-gather.6
  195.1 156.0 all-gather.8
  353.0 167.3 all-gather.10
Sparse Core Ops, SparseCore 1:
  56.8 867.8 reduce-scatter.1
where the time goes:
time: 933 us; the launch traced here: 932 us
  waiting for transfers between devices  740 us (79%)
  starting transfers between devices  69.1 us (7%)
  matrix products  59.6 us (6%)
  local copies, waits for them, and re-layouts  35 us (4%)
  between operations  15.7 us (2%)
  other arithmetic  12.3 us (1%)
    reduce_scatter x1, waiting for transfers between devices, body(): lax.psum_scatter(lax.dot_general(attn_local, latent_local, (((0,), (0,)),...  220 us
    all_gather x1, waiting for transfers between devices, body(): lax.all_gather(down_part, 'dp', axis=0, tiled=True)  163 us
    all_gather x1, waiting for transfers between devices, body(): lax.all_gather(up_part, 'dp', axis=1, tiled=True)  152 us
    all_gather x1, waiting for transfers between devices, body(): lax.all_gather(gate_part, 'dp', axis=1, tiled=True)  80.1 us
    all_to_all x1, starting transfers between devices, body(): lax.all_to_all(ret_inner, 'expert', split_axis=0, concat_axis=0, tiled=True)  39 us
    ppermute x1, waiting for transfers between devices, shifted(): lax.ppermute(array, axis, [(i, (i + by) % peers) for i in range(peers)])  27.5 us
    all_to_all x1, waiting for transfers between devices, body(): lax.all_to_all(ret_back, 'expert', split_axis=0, concat_axis=0, tiled=True)  22.4 us
    all_to_all x1, waiting for transfers between devices, body(): lax.all_to_all(sent_fwd, 'expert', split_axis=0, concat_axis=0, tiled=True)  21.9 us
  transfers between devices with their start and end apart: 11, of which 10 were waited for; matrix products, arithmetic and copies ran while one was open for 11% of the time, Pallas kernels for 0%

commit v1 on v0

v1 whole, which is shorter than its diff:
```python
import functools

import jax
import jax.numpy as jnp
import numpy as np
from jax import lax
from jax.experimental import pallas as pl
from jax.experimental.pallas import tpu as pltpu
from jax.sharding import PartitionSpec as P

TOP = 2
ROUTE_SCALE = 2.5
CAP = 6
TOK = 64
D = 3584
EXPERTS = 32
HALF = 512
LATENT = 512
Q = 4
PIECE = D // Q
S = 7
PART = D // S
SLOT = 2 * CAP * Q
WIRE = EXPERTS * SLOT
ROWS = EXPERTS * CAP
CHUNK = 8
KV_ROWS = 56
MESH = pl.DeviceIdType.MESH
BF = jnp.bfloat16
F32 = jnp.float32

STEPS = [(2, 2), (1, 0), (3, 0), (0, 1), (0, 3), (2, 0), (0, 2), (1, 1), (3, 3), (1, 3), (3, 1), (2, 1), (1, 2), (2, 3), (3, 2)]
STEPS_X = sum(x * 4**i for i, (x, _) in enumerate(STEPS))
STEPS_Y = sum(y * 4**i for i, (_, y) in enumerate(STEPS))


def permutations():
    unpack = np.zeros((CHUNK * SLOT, CHUNK * SLOT), np.float32)
    pack_part = np.zeros((CHUNK * SLOT, S * CHUNK * CAP), np.float32)
    pack_inner = np.zeros((EXPERTS * 16, 2 * ROWS), np.float32)
    for s in range(CHUNK):
        for slot in range(CAP):
            for q in range(Q):
                for j in range(2):
                    unpack[j * 192 + q * 48 + s * CAP + slot, s * SLOT + q * 12 + j * CAP + slot] = 1
            for q in range(S):
                pack_part[s * SLOT + q * CAP + slot, q * 48 + s * CAP + slot] = 1
    for s in range(EXPERTS):
        for j in range(2):
            for slot in range(CAP):
                pack_inner[s * 16 + j * CAP + slot, j * ROWS + s * CAP + slot] = 1
    return unpack, unpack.T.copy(), pack_part, pack_inner


def dot(a, b):
    return jnp.dot(a, b, preferred_element_type=F32)


def dot_nt(a, b):
    return lax.dot_general(a, b, (((1,), (1,)), ((), ())), preferred_element_type=F32)


def kernel(
    xf, xb, cg, meta, router, unpack, pack, pack_part, pack_inner,
    gate_hbm, up_hbm, down_hbm, attn_hbm, latent_hbm,
    fwd_out, bwd_out, kv_out,
    gate, up, down, stack_f, stack_own, stack_peer, meta_peer,
    w1, w2, w3, a1, a2, a3, x2, gg, gu, hid, inner,
    fo_own, fo_peer, fo_got, back, a4, a5, part,
    iv_wire, iv_got, g_fwd, g_bwd, acc, peer_part, peer_got, val, val_send, val_got,
    attn_got, latent_got, kv_sum, kv_got, y_send, dx_send, y_got, dx_got,
    load_sem, z_send, z_recv, u_send, u_recv, local_sem, p_send, p_recv,
):
    pi, dp, ex = lax.axis_index("pipe"), lax.axis_index("dp"), lax.axis_index("expert")
    core = lax.rem(ex, 2)
    px = lax.rem(lax.div(ex, 2), 4)
    py = lax.div(ex, 8)
    zpeer = (pi, 1 - dp, ex)
    ahead = (lax.rem(pi + 1, 4), dp, ex)
    behind = (lax.rem(pi + 3, 4), dp, ex)

    loads = [
        pltpu.make_async_copy(src, dst, load_sem.at[i])
        for i, (src, dst) in enumerate([(gate_hbm, gate), (up_hbm, up), (down_hbm, down)])
    ]

    barrier = pltpu.get_barrier_semaphore()
    pl.semaphore_signal(barrier, inc=1, device_id=zpeer, device_id_type=MESH)
    pl.semaphore_signal(barrier, inc=1, device_id=ahead, device_id_type=MESH)
    pl.semaphore_signal(barrier, inc=1, device_id=behind, device_id_type=MESH)

    def greet(o, c):
        pl.semaphore_signal(barrier, inc=1, device_id=(pi, dp, lax.rem(ex + o, EXPERTS)), device_id_type=MESH)
        return c

    lax.fori_loop(1, EXPERTS, greet, 0)
    for load in loads:
        load.start()

    def plane(unit, src, dst, rows, one_source=False, cols=None):
        def piece(e):
            at = pl.ds(pl.multiple_of(e * rows, 16), rows)
            if one_source:
                return src
            return src.at[at] if cols is None else src.at[at, pl.ds(0, cols)]

        def copy(i, dx, dy, dc):
            to = (lax.rem(py + dy, 4) * 4 + lax.rem(px + dx, 4)) * 2 + lax.rem(core + dc, 2)
            return pltpu.make_async_remote_copy(
                src_ref=piece(to),
                dst_ref=dst.at[pl.ds(pl.multiple_of(ex * rows, 16), rows)],
                send_sem=u_send.at[unit, i],
                recv_sem=u_recv.at[unit, i],
                device_id=(pi, dp, to),
                device_id_type=MESH,
            )

        def local():
            return pltpu.make_async_copy(
                piece(ex),
                dst.at[pl.ds(pl.multiple_of(ex * rows, 16), rows)],
                local_sem.at[unit],
            )

        def start():
            def step(i, c):
                tx, ty = c
                dx, dy = lax.rem(tx, 4), lax.rem(ty, 4)
                copy(2 * i, dx, dy, 0).start()
                copy(2 * i + 1, dx, dy, 1).start()
                return lax.div(tx, 4), lax.div(ty, 4)

            lax.fori_loop(0, 15, step, (jnp.int32(STEPS_X), jnp.int32(STEPS_Y)))
            copy(30, 0, 0, 1).start()
            local().start()

        def wait_recv():
            def step(i, c):
                pltpu.make_async_copy(dst.at[pl.ds(0, rows)], dst.at[pl.ds(0, rows)], u_recv.at[unit, i]).wait()
                return c

            lax.fori_loop(0, 31, step, 0)
            local().wait()

        def wait_send():
            def step(i, c):
                pltpu.make_async_copy(dst.at[pl.ds(0, rows)], dst.at[pl.ds(0, rows)], u_send.at[unit, i]).wait()
                return c

            lax.fori_loop(0, 31, step, 0)

        return start, wait_recv, wait_send

    def to_zpeer(i, src, dst):
        return pltpu.make_async_remote_copy(
            src_ref=src, dst_ref=dst, send_sem=z_send.at[i], recv_sem=z_recv.at[i], device_id=zpeer, device_id_type=MESH
        )

    def place(code_a, code_b, stack, wire):
        first = jnp.concatenate([code_a[0:1], code_b[0:1] + float(CAP)], axis=1).astype(jnp.int32)
        second = jnp.concatenate([code_a[1:2], code_b[1:2] + float(CAP)], axis=1).astype(jnp.int32)

        def step(g, c):
            row = lax.broadcasted_iota(jnp.int32, (192, 512), 0) + g * 192
            member = jnp.where((row == first) | (row == second), 1.0, 0.0).astype(BF)
            wire[pl.ds(pl.multiple_of(g * 192, 16), 192), :] = dot(member, stack[...]).astype(BF)
            return c

        lax.fori_loop(0, 8, step, 0)

    def unpacked(wire):
        def step(c, carry):
            rows = dot(unpack[...], wire[pl.ds(pl.multiple_of(c * 384, 16), 384), :]).astype(BF)
            for j in range(2):
                for q in range(Q):
                    x2[pl.ds(pl.multiple_of(j * ROWS + c * 48, 16), 48), q * PIECE : (q + 1) * PIECE] = rows[
                        j * 192 + q * 48 : j * 192 + (q + 1) * 48
                    ]
            return carry

        lax.fori_loop(0, 4, step, 0)

    for q in range(Q):
        cols = slice(q * PIECE, (q + 1) * PIECE)
        stack_f[q * TOK : (q + 1) * TOK, :] = xf[:, cols]
        stack_own[q * TOK : (q + 1) * TOK, :] = xb[:, cols]
        stack_own[256 + q * TOK : 256 + (q + 1) * TOK, :] = cg[:, cols]
    own = meta[...]
    place(own[2:4], own[2:4], stack_own, w1)

    pl.semaphore_wait(barrier, 34)
    z_meta = to_zpeer(0, meta, meta_peer)
    z_f = to_zpeer(1, stack_f.at[pl.ds(0, 256)], stack_f.at[pl.ds(256, 256)])
    z_xg = to_zpeer(2, stack_own, stack_peer)
    z_meta.start()
    z_f.start()
    start1, recv1, sent1 = plane(0, w1, a1, SLOT)
    start1()
    z_meta.wait_recv()
    peer = meta_peer[...]
    z_f.wait_recv()
    z_xg.start()
    place(own[0:2], peer[0:2], stack_f, w2)
    start2, recv2, sent2 = plane(1, w2, a2, SLOT)
    start2()

    own_t, peer_t = own.T, peer.T

    def split(values):
        hi = values.astype(BF)
        return hi, (values - hi.astype(F32)).astype(BF)

    lane = lax.broadcasted_iota(jnp.int32, (TOK, WIRE), 1)

    def gate_rows(code0, code1, gate0, gate1, offset):
        value = jnp.where(lane == code0.astype(jnp.int32) + offset, gate0, 0.0)
        value = value + jnp.where(lane == code1.astype(jnp.int32) + offset, gate1, 0.0)
        return split(value)

    for j, m in enumerate((own_t, peer_t)):
        for q in range(Q):
            m_q = m[q * TOK : (q + 1) * TOK]
            hi, lo = gate_rows(m_q[:, 2:3], m_q[:, 3:4], m_q[:, 4:5], m_q[:, 5:6], j * CAP)
            g_bwd[j * 512 + q * TOK : j * 512 + (q + 1) * TOK, :] = hi
            g_bwd[j * 512 + 256 + q * TOK : j * 512 + 256 + (q + 1) * TOK, :] = lo
    for q in range(S):
        m = own_t[0:TOK]
        hi, lo = gate_rows(m[:, 0:1], m[:, 1:2], m[:, 8:9], m[:, 9:10], q * CAP)
        g_fwd[q * TOK : (q + 1) * TOK, :] = hi
        g_fwd[S * TOK + q * TOK : S * TOK + (q + 1) * TOK, :] = lo

    def backward(j):
        total = jnp.zeros((ROWS, 1), F32)
        for n in range(HALF // 256):
            cols = slice(n * 256, (n + 1) * 256)
            gate_act = dot(x2[0:ROWS, :], gate[:, cols])
            up_act = dot(x2[0:ROWS, :], up[:, cols])
            grad_hidden = dot_nt(x2[ROWS : 2 * ROWS, :], down[cols, :])
            sig = jax.nn.sigmoid(gate_act)
            active = gate_act * sig
            hidden = (active * up_act).astype(BF).astype(F32)
            total = total + jnp.sum(hidden * grad_hidden, axis=1, keepdims=True)
            gg[:, cols] = (grad_hidden * up_act * sig * (1.0 + gate_act * (1.0 - sig))).astype(BF)
            gu[:, cols] = (grad_hidden * active).astype(BF)
        hi, lo = split(total)
        side = lax.broadcasted_iota(jnp.int32, (ROWS, 128), 1) < 64
        inner[j * ROWS : (j + 1) * ROWS, :] = jnp.where(side, hi.astype(F32), lo.astype(F32)).astype(BF)

        def step(q, c):
            cols = pl.ds(pl.multiple_of(q * PIECE, 128), PIECE)
            rows = (dot_nt(gg[...], gate[cols, :]) + dot_nt(gu[...], up[cols, :])).astype(BF)
            for g in range(4):
                back[pl.ds(pl.multiple_of(g * 384 + j * 192 + q * 48, 16), 48), :] = rows[g * 48 : (g + 1) * 48]
            return c

        lax.fori_loop(0, Q, step, 0)

    z_xg.wait_recv()
    place(peer[2:4], peer[2:4], stack_peer, w3)
    start3, recv3, sent3 = plane(2, w3, a3, SLOT)
    start3()

    for load in loads:
        load.wait()
    recv1()
    unpacked(a1)
    backward(0)

    recv2()
    unpacked(a2)
    for n in range(HALF // 256):
        cols = slice(n * 256, (n + 1) * 256)
        gate_act = dot(x2[...], gate[:, cols])
        up_act = dot(x2[...], up[:, cols])
        hid[:, cols] = (gate_act * jax.nn.sigmoid(gate_act) * up_act).astype(BF)

    def forward(q, c):
        cols = pl.ds(pl.multiple_of(q * PIECE, 128), PIECE)
        rows = dot(hid[...], down[:, cols]).astype(BF)
        fo_own[:, cols] = rows[0:ROWS]
        fo_peer[:, cols] = rows[ROWS : 2 * ROWS]
        return c

    lax.fori_loop(0, Q, forward, 0)
    z_out = to_zpeer(3, fo_peer, fo_got)
    z_out.start()

    recv3()
    unpacked(a3)
    backward(1)
    sent1()

    def pack_back(g, c):
        rows = pl.ds(pl.multiple_of(g * 384, 16), 384)
        w1[rows, :] = dot(pack[...], back[rows, :]).astype(BF)
        return c

    lax.fori_loop(0, 4, pack_back, 0)
    iv_wire[...] = dot(pack_inner[...], inner[...]).astype(BF)
    start4, recv4, sent4 = plane(3, w1, a4, SLOT)
    start_i, recv_i, sent_i = plane(4, iv_wire, iv_got, 16)
    start_i()
    start4()

    z_out.wait_recv()
    sent2()

    def pack_forward(g, c):
        rows = pl.ds(pl.multiple_of(g * 48, 16), 48)
        for q in range(S):
            cols = slice(q * PART, (q + 1) * PART)
            part[q * 48 : (q + 1) * 48, :] = (fo_own[rows, cols].astype(F32) + fo_got[rows, cols].astype(F32)).astype(BF)
        w2[pl.ds(pl.multiple_of(g * 384, 16), 384), 0:PART] = dot(pack_part[...], part[...]).astype(BF)
        return c

    lax.fori_loop(0, 4, pack_forward, 0)
    start5, recv5, sent5 = plane(5, w2, a5, SLOT, cols=PART)
    start5()
    start_a, recv_a, sent_a = plane(6, attn_hbm, attn_got, TOK)
    start_l, recv_l, sent_l = plane(7, latent_hbm, latent_got, TOK, one_source=True)
    start_a()
    start_l()

    recv_i()
    lane_i = lax.broadcasted_iota(jnp.int32, (TOK, EXPERTS * 16), 1)
    picks = []
    for j, m in enumerate((own_t, peer_t)):
        for k in range(TOP):
            code = m[0:TOK, 6 + k : 7 + k].astype(jnp.int32) + j * CAP
            picks.append(jnp.where(lane_i == code, 1.0, 0.0).astype(BF))
    val[...] = dot(jnp.concatenate(picks, axis=0), iv_got[...])
    val_send[...] = val[128:256, :].astype(BF)
    recv4()
    got = dot(g_bwd[512:1024, :], a4[...])
    peer_part[...] = (got[0:256] + got[256:512]).astype(BF)
    z_val = to_zpeer(4, val_send, val_got)
    z_part = to_zpeer(5, peer_part, peer_got)
    z_val.start()
    z_part.start()
    got = dot(g_bwd[0:512, :], a4[...])
    acc[...] = got[0:256] + got[256:512]

    def to_next(i, src, dst):
        return pltpu.make_async_remote_copy(
            src_ref=src, dst_ref=dst, send_sem=p_send.at[i], recv_sem=p_recv.at[i], device_id=ahead, device_id_type=MESH
        )

    recv5()
    got = dot(g_fwd[...], a5[...])
    for q in range(S):
        cols = slice(q * PART, (q + 1) * PART)
        y = xf[:, cols].astype(F32) + got[q * TOK : (q + 1) * TOK] + got[(S + q) * TOK : (S + q + 1) * TOK]
        y_send[:, cols] = y.astype(BF)
    n_y = to_next(0, y_send, y_got)
    n_y.start()

    z_val.wait_recv()
    inner0 = val[0:64, 0:1] + val[0:64, 64:65] + val_got[0:64, 0:1].astype(F32) + val_got[0:64, 64:65].astype(F32)
    inner1 = val[64:128, 0:1] + val[64:128, 64:65] + val_got[64:128, 0:1].astype(F32) + val_got[64:128, 64:65].astype(F32)
    m = own_t[0:TOK]
    rate0, rate1, rate_total = m[:, 10:11], m[:, 11:12], m[:, 12:13]
    weighted = (inner0 * rate0 + inner1 * rate1) / (rate_total * rate_total)
    logit0 = ROUTE_SCALE * (inner0 / rate_total - weighted) * rate0 * (1.0 - rate0)
    logit1 = ROUTE_SCALE * (inner1 / rate_total - weighted) * rate1 * (1.0 - rate1)
    lane_e = lax.broadcasted_iota(jnp.int32, (TOK, EXPERTS), 1)
    dlogits = jnp.where(lane_e == m[:, 13:14].astype(jnp.int32), logit0, 0.0)
    dlogits = (dlogits + jnp.where(lane_e == m[:, 14:15].astype(jnp.int32), logit1, 0.0)).astype(BF)
    for q in range(Q):
        cols = slice(q * PIECE, (q + 1) * PIECE)
        rows = slice(q * TOK, (q + 1) * TOK)
        acc[rows, :] = acc[rows, :] + dot_nt(dlogits, router[cols, :]) + cg[:, cols].astype(F32)
    z_part.wait_recv()
    for q in range(Q):
        rows = slice(q * TOK, (q + 1) * TOK)
        dx_send[:, q * PIECE : (q + 1) * PIECE] = (acc[rows, :] + peer_got[rows, :].astype(F32)).astype(BF)
    n_dx = to_next(1, dx_send, dx_got)
    n_dx.start()

    recv_a()
    recv_l()
    kv_sum[...] = lax.dot_general(attn_got[...], latent_got[...], (((0,), (0,)), ((), ())), preferred_element_type=F32)
    z_kv = to_zpeer(6, kv_sum.at[pl.ds(pl.multiple_of((1 - dp) * 64, 8), KV_ROWS)], kv_got)
    z_kv.start()
    z_kv.wait_recv()
    kv_out[...] = kv_sum[pl.ds(pl.multiple_of(dp * 64, 8), KV_ROWS), :] + kv_got[...]

    n_y.wait_recv()
    fwd_out[...] = y_got[...]
    n_dx.wait_recv()
    bwd_out[...] = dx_got[...]

    for sent in (sent3, sent4, sent_i, sent5, sent_a, sent_l):
        sent()
    for copy in (z_meta, z_f, z_xg, z_out, z_val, z_part, z_kv, n_y, n_dx):
        copy.wait_send()


def slot_keys(routes):
    flat = routes.reshape(TOK * TOP)
    member = (flat[:, None] == jnp.arange(EXPERTS, dtype=jnp.int32)[None, :]).astype(jnp.int32)
    earlier = jnp.cumsum(member, axis=0) - member
    return jnp.sum(earlier * member, axis=1).reshape(routes.shape)


def route_gates(tokens, router, routes):
    logits = jnp.dot(tokens, router, preferred_element_type=F32)
    table = (routes[:, :, None] == jnp.arange(EXPERTS, dtype=jnp.int32)[None, None, :]).astype(F32)
    rates = jax.nn.sigmoid(jnp.sum(logits[:, None, :] * table, axis=2))
    total = jnp.sum(rates, axis=1, keepdims=True)
    return ROUTE_SCALE * rates / total, rates, total


def body(x_fwd, routes_fwd, x_bwd, cot_bwd, routes_bwd, router_weight, gate_weight, up_weight, down_weight, attn_input, latent_cot):
    router = router_weight[0]
    rf, rb = routes_fwd[0], routes_bwd[0]
    slot_f, slot_b = slot_keys(rf), slot_keys(rb)
    gates_f, _, _ = route_gates(x_fwd[0], router, rf)
    gates_b, rates_b, total_b = route_gates(x_bwd[0], router, rb)
    offsets = jnp.repeat(jnp.arange(Q, dtype=F32) * 12, TOK)[None, :]

    def rows(values):
        return jnp.tile(values.astype(F32).T, (1, Q))

    meta = jnp.concatenate(
        [
            rows(rf * SLOT + slot_f) + offsets,
            rows(rb * SLOT + slot_b) + offsets,
            rows(gates_b),
            rows(rb * 16 + slot_b),
            rows(gates_f),
            rows(rates_b),
            rows(total_b),
            rows(rb),
            jnp.zeros((1, Q * TOK), F32),
        ],
        axis=0,
    )
    attn = attn_input[0].reshape(TOK, 2, EXPERTS, KV_ROWS).transpose(2, 0, 1, 3)
    attn = jnp.pad(attn, ((0, 0), (0, 0), (0, 0), (0, 64 - KV_ROWS))).reshape(EXPERTS * TOK, 128)
    consts = [jnp.asarray(c, BF) for c in permutations()]
    vmem = pl.BlockSpec(memory_space=pltpu.VMEM)
    anywhere = pl.BlockSpec(memory_space=pl.ANY)
    V = pltpu.VMEM
    dma = pltpu.SemaphoreType.DMA
    scratch = [
        V((D, HALF), BF), V((D, HALF), BF), V((HALF, D), BF),
        V((512, PIECE), BF), V((512, PIECE), BF), V((512, PIECE), BF), V((16, Q * TOK), F32),
        V((WIRE, PIECE), BF), V((WIRE, PIECE), BF), V((WIRE, PIECE), BF),
        V((WIRE, PIECE), BF), V((WIRE, PIECE), BF), V((WIRE, PIECE), BF),
        V((2 * ROWS, D), BF), V((ROWS, HALF), BF), V((ROWS, HALF), BF), V((2 * ROWS, HALF), BF), V((2 * ROWS, 128), BF),
        V((ROWS, D), BF), V((ROWS, D), BF), V((ROWS, D), BF),
        V((WIRE, PIECE), BF), V((WIRE, PIECE), BF),
        V((WIRE, PART), BF), V((S * 48, PART), BF),
        V((EXPERTS * 16, 128), BF), V((EXPERTS * 16, 128), BF),
        V((2 * S * TOK, WIRE), BF), V((1024, WIRE), BF),
        V((256, PIECE), F32), V((256, PIECE), BF), V((256, PIECE), BF),
        V((256, 128), F32), V((128, 128), BF), V((128, 128), BF),
        V((EXPERTS * TOK, 128), BF), V((EXPERTS * TOK, LATENT), BF), V((128, LATENT), F32), V((KV_ROWS, LATENT), F32),
        V((TOK, D), BF), V((TOK, D), BF), V((TOK, D), BF), V((TOK, D), BF),
        dma((3,)), dma((7,)), dma((7,)), dma((8, 31)), dma((8, 31)), dma((8,)), dma((2,)), dma((2,)),
    ]
    fwd, bwd, kv = pl.pallas_call(
        kernel,
        out_shape=[
            jax.ShapeDtypeStruct((TOK, D), BF),
            jax.ShapeDtypeStruct((TOK, D), BF),
            jax.ShapeDtypeStruct((KV_ROWS, LATENT), F32),
        ],
        in_specs=[vmem] * 9 + [anywhere] * 5,
        out_specs=[vmem] * 3,
        scratch_shapes=scratch,
        compiler_params=pltpu.CompilerParams(collective_id=0, has_side_effects=True, vmem_limit_bytes=63 * 2**20),
        name="layer",
    )(
        x_fwd[0], x_bwd[0], cot_bwd[0], meta, router, *consts,
        gate_weight[0, 0], up_weight[0, 0], down_weight[0, 0], attn, latent_cot[0],
    )
    return fwd[None], bwd[None], kv[None]


def solution(mesh):
    tokens = P("pipe", ("dp", "expert"), None)
    in_specs = (
        tokens, tokens, tokens, tokens, tokens,
        P("pipe", None, None),
        P("pipe", "expert", None, "dp"),
        P("pipe", "expert", None, "dp"),
        P("pipe", "expert", "dp", None),
        tokens, tokens,
    )
    return jax.shard_map(body, mesh=mesh, in_specs=in_specs, out_specs=(tokens,) * 3, check_vma=False)
```

time: 933 us -> 274 us (0.29)
  the two profiles are of different devices: /device:TPU:32 before, /device:TPU:176 now
where the time goes in v1:
time: 274 us
  Pallas kernels  249 us (91%)
  local copies, waits for them, and re-layouts  17.5 us (6%)
  other arithmetic  4.46 us (2%)
    pallas_call x1, Pallas kernels, body(): pl.pallas_call(kernel, out_shape=[jax.ShapeDtypeStruct((TOK, D), BF), jax...  249 us
    unnamed x9, local copies, waits for them, and re-layouts  9.06 us

profile of v1, /device:TPU:176, one launch (start us, length us, event | category | flops | bytes accessed | tf_op | source)
XLA Modules:
  0.0 273.8 jit_solution(5504457650017310410)
XLA Ops:
  0.6 1.3 fusion
  1.9 0.7 select_reduce_fusion.2
  2.7 1.3 fusion.2
  4.0 0.7 select_reduce_fusion.3
  4.7 0.1 tile.37
  4.8 0.8 copy.42
  5.6 0.1 eq.60
  5.7 0.1 fusion.4
  5.8 0.2 reduce_window_sum.18
  6.0 0.2 select_reduce_fusion
  6.2 0.1 reshape.59
  6.3 0.1 copy.43
  6.4 0.7 convert_bitcast_fusion.1
  7.1 0.1 tile.35
  7.2 0.8 copy.40
  8.0 0.1 eq.56
  8.1 0.1 fusion.5
  8.2 0.2 reduce_window_sum.17
  8.4 0.2 select_reduce_fusion.1
  8.5 0.1 reshape.58
  8.7 0.1 copy.41
  8.8 0.7 convert_bitcast_fusion.3
  9.5 0.1 tile.33
  9.6 0.1 broadcast_in_dim.12
  9.6 0.1 add.43
  9.7 0.1 tile.80
  9.8 0.1 tile.82
  9.9 0.0 copy-start
  9.9 0.1 tile.84
  10.0 0.1 tile.78
  10.1 0.7 convert_bitcast_fusion
  10.8 0.1 tile.86
  10.9 1.2 concatenate.3.meta
  12.1 3.1 %reshape_squeeze.3 = bf16[64,2,32,56]{3,2,1,0:T(8,128)(2,1)S(1)} reshape(bf16[1,64,3584]{2,1,0:T(8,128)(2,1)} %param.24) | data formatting | bytes 917504 | tf_op jit(solution)/shard_map/reshape;squeeze | solution.py:438
  15.2 1.1 copy.47
  16.3 1.2 pad.4.clone
  17.6 1.3 reshape.60.attn_hbm
  18.8 0.0 copy-done
  18.8 1.2 copy.44
  20.1 248.5 %layer.1 = (bf16[64,3584]{1,0:T(8,128)(2,1)}, bf16[64,3584]{1,0:T(8,128)(2,1)}, f32[56,512]{1,0:T(8,128)}) custom-call(bf16[64,3584]{1,0:T(8,128)(2,1)} %bitcast.45, bf16[64,3584]{1,0:T(8,128)(2,1)} %bitcast.46, bf16[64,3584]{1,0:T(8,128)(2,1)} %bitcast.49, f32[16,256]{1,0:T(8,128)} %concatenate.3.meta, bf16[3584,32]{1,0:T(8,128)(2,1)} %bitcast.44, ...), custom_call_target="tpu_custom_call" | custom-call | tf_op jit(solution)/shard_map/layer/pallas_call | solution.py:462
  268.6 1.8 copy.51
  270.4 1.8 copy.52
  272.2 1.6 copy.53
  (14 shorter events, 0.1 us)
Async XLA Ops:
  9.9 8.9 %copy-start = (bf16[1,3584,32]{1,2,0:T(8,128)(2,1)S(1)}, bf16[1,3584,32]{1,2,0:T(8,128)(2,1)}, u32[]{:S(2)}) copy-start(bf16[1,3584,32]{1,2,0:T(8,128)(2,1)} %param.20) | copy-start | bytes 688132

commit v2 on v1

v2 whole, which is shorter than its diff:
```python
import functools

import jax
import jax.numpy as jnp
import numpy as np
from jax import lax
from jax.experimental import pallas as pl
from jax.experimental.pallas import tpu as pltpu
from jax.sharding import PartitionSpec as P

TOP = 2
ROUTE_SCALE = 2.5
CAP = 6
TOK = 64
D = 3584
EXPERTS = 32
HALF = 512
LATENT = 512
Q = 4
PIECE = D // Q
S = 7
PART = D // S
SLOT = 2 * CAP * Q
WIRE = EXPERTS * SLOT
ROWS = EXPERTS * CAP
CHUNK = 8
KV_ROWS = 56
MESH = pl.DeviceIdType.MESH
BF = jnp.bfloat16
F32 = jnp.float32

STEPS = [(2, 2), (1, 0), (3, 0), (0, 1), (0, 3), (2, 0), (0, 2), (1, 1), (3, 3), (1, 3), (3, 1), (2, 1), (1, 2), (2, 3), (3, 2)]
STEPS_X = sum(x * 4**i for i, (x, _) in enumerate(STEPS))
STEPS_Y = sum(y * 4**i for i, (_, y) in enumerate(STEPS))


def permutations():
    unpack = np.zeros((CHUNK * SLOT, CHUNK * SLOT), np.float32)
    pack_part = np.zeros((CHUNK * SLOT, S * CHUNK * CAP), np.float32)
    pack_inner = np.zeros((EXPERTS * 16, ROWS), np.float32)
    for s in range(CHUNK):
        for slot in range(CAP):
            for q in range(Q):
                for j in range(2):
                    unpack[j * 192 + q * 48 + s * CAP + slot, s * SLOT + q * 12 + j * CAP + slot] = 1
            for q in range(S):
                pack_part[s * SLOT + q * CAP + slot, q * 48 + s * CAP + slot] = 1
    for s in range(EXPERTS):
        for slot in range(CAP):
            pack_inner[s * 16 + slot, s * CAP + slot] = 1
    return unpack, unpack.T.copy(), pack_part, pack_inner


def dot(a, b):
    return jnp.dot(a, b, preferred_element_type=F32)


def dot_nt(a, b):
    return lax.dot_general(a, b, (((1,), (1,)), ((), ())), preferred_element_type=F32)


def kernel(
    xf, xb, cg, routes_f, routes_b, attn, latent, router, unpack, pack, pack_part, pack_inner,
    gate_hbm, up_hbm, down_hbm,
    fwd_out, bwd_out, kv_out,
    gate, up, down, stack_f, stack_own, stack_peer, meta, meta_peer, cols_own, cols_peer,
    w1, w2, a1, a2, a3, x2, gg, gu, hid, inner, inner_got, inner_sum,
    back_own, back_peer, back_got, fwd_rows, a4, a5, part,
    iv_wire, iv_got, g_part, g_pair, acc, peer_part, peer_got,
    attn_wire, attn_got, latent_got, kv_sum, kv_got, y_send, dx_send, y_got, dx_got,
    load_sem, z_send, z_recv, u_send, u_recv, local_sem, l_send, l_recv, p_send, p_recv,
):
    pi, dp, ex = lax.axis_index("pipe"), lax.axis_index("dp"), lax.axis_index("expert")
    core = lax.rem(ex, 2)
    px = lax.rem(lax.div(ex, 2), 4)
    py = lax.div(ex, 8)
    zpeer = (pi, 1 - dp, ex)
    ahead = (lax.rem(pi + 1, 4), dp, ex)
    behind = (lax.rem(pi + 3, 4), dp, ex)

    loads = [
        pltpu.make_async_copy(src, dst, load_sem.at[i])
        for i, (src, dst) in enumerate([(gate_hbm, gate), (up_hbm, up), (down_hbm, down)])
    ]

    barrier = pltpu.get_barrier_semaphore()
    pl.semaphore_signal(barrier, inc=1, device_id=zpeer, device_id_type=MESH)
    pl.semaphore_signal(barrier, inc=1, device_id=ahead, device_id_type=MESH)
    pl.semaphore_signal(barrier, inc=1, device_id=behind, device_id_type=MESH)

    def greet(o, c):
        pl.semaphore_signal(barrier, inc=1, device_id=(pi, dp, lax.rem(ex + o, EXPERTS)), device_id_type=MESH)
        return c

    lax.fori_loop(1, EXPERTS, greet, 0)
    for load in loads:
        load.start()

    def plane(unit, src, dst, rows, place_at, cols=None):
        def piece(e):
            at = pl.ds(pl.multiple_of(e * rows, 16), rows)
            return src.at[at] if cols is None else src.at[at, pl.ds(0, cols)]

        def copy(i, dx, dy, dc):
            to = (lax.rem(py + dy, 4) * 4 + lax.rem(px + dx, 4)) * 2 + lax.rem(core + dc, 2)
            return pltpu.make_async_remote_copy(
                src_ref=piece(to),
                dst_ref=dst.at[pl.ds(pl.multiple_of(place_at * rows, 16), rows)],
                send_sem=u_send.at[unit, i],
                recv_sem=u_recv.at[unit, i],
                device_id=(pi, dp, to),
                device_id_type=MESH,
            )

        def local():
            return pltpu.make_async_copy(
                piece(ex),
                dst.at[pl.ds(pl.multiple_of(place_at * rows, 16), rows)],
                local_sem.at[unit],
            )

        def start():
            def step(i, c):
                tx, ty = c
                dx, dy = lax.rem(tx, 4), lax.rem(ty, 4)
                copy(2 * i, dx, dy, 0).start()
                copy(2 * i + 1, dx, dy, 1).start()
                return lax.div(tx, 4), lax.div(ty, 4)

            lax.fori_loop(0, 15, step, (jnp.int32(STEPS_X), jnp.int32(STEPS_Y)))
            copy(30, 0, 0, 1).start()
            local().start()

        def wait_recv():
            def step(i, c):
                pltpu.make_async_copy(dst.at[pl.ds(0, rows)], dst.at[pl.ds(0, rows)], u_recv.at[unit, i]).wait()
                return c

            lax.fori_loop(0, 31, step, 0)
            local().wait()

        def wait_send():
            def step(i, c):
                pltpu.make_async_copy(dst.at[pl.ds(0, rows)], dst.at[pl.ds(0, rows)], u_send.at[unit, i]).wait()
                return c

            lax.fori_loop(0, 31, step, 0)

        return start, wait_recv, wait_send

    def to_zpeer(i, src, dst):
        return pltpu.make_async_remote_copy(
            src_ref=src, dst_ref=dst, send_sem=z_send.at[i], recv_sem=z_recv.at[i], device_id=zpeer, device_id_type=MESH
        )

    def place(code_a, code_b, stack, wire):
        first = jnp.concatenate([code_a[0:1], code_b[0:1] + float(CAP)], axis=1).astype(jnp.int32)
        second = jnp.concatenate([code_a[1:2], code_b[1:2] + float(CAP)], axis=1).astype(jnp.int32)

        def step(g, c):
            row = lax.broadcasted_iota(jnp.int32, (192, 512), 0) + g * 192
            member = jnp.where((row == first) | (row == second), 1.0, 0.0).astype(BF)
            wire[pl.ds(pl.multiple_of(g * 192, 16), 192), :] = dot(member, stack[...]).astype(BF)
            return c

        lax.fori_loop(0, 8, step, 0)

    def unpacked(wire):
        def step(c, carry):
            rows = dot(unpack[...], wire[pl.ds(pl.multiple_of(c * 384, 16), 384), :]).astype(BF)
            for j in range(2):
                for q in range(Q):
                    x2[pl.ds(pl.multiple_of(j * ROWS + c * 48, 16), 48), q * PIECE : (q + 1) * PIECE] = rows[
                        j * 192 + q * 48 : j * 192 + (q + 1) * 48
                    ]
            return carry

        lax.fori_loop(0, 4, step, 0)

    lane = lax.broadcasted_iota(jnp.int32, (TOK, 128), 1)

    def columns(values):
        out = jnp.zeros((TOK, 128), F32)
        for i, v in enumerate(values):
            out = jnp.where(lane == i, v, out)
        return out

    same_token = lax.broadcasted_iota(jnp.int32, (TOK, Q * TOK), 1) & (TOK - 1)
    same_token = jnp.where(same_token == lax.broadcasted_iota(jnp.int32, (TOK, Q * TOK), 0), 1.0, 0.0).astype(BF)
    named, named_rows = [], []
    for routes in (routes_f, routes_b):
        values = routes[...].astype(F32).astype(BF)
        turned = dot_nt(same_token[:, 0:TOK], values)
        tiled = dot(values, same_token)
        for k in range(TOP):
            named.append(turned[:, k : k + 1])
            named_rows.append(tiled[k : k + 1])
    lane_q = lax.broadcasted_iota(jnp.int32, (TOK, Q * TOK), 1)
    before = lax.broadcasted_iota(jnp.int32, (TOK, Q * TOK), 0) < (lane_q & (TOK - 1))
    offset = ((lane_q[0:1] >> 6) * 12).astype(F32)
    for i in range(4):
        row = named_rows[i]
        same = (named[i // 2 * 2] == row) | (named[i // 2 * 2 + 1] == row)
        slot = jnp.sum(jnp.where(same & before, 1.0, 0.0), axis=0, keepdims=True)
        meta[i : i + 1, :] = row * float(SLOT) + slot + offset
        if i >= 2:
            meta[i + 2 : i + 3, :] = row * 16.0 + slot
            meta[i + 4 : i + 5, :] = row

    for q in range(Q):
        cols = slice(q * PIECE, (q + 1) * PIECE)
        stack_f[q * TOK : (q + 1) * TOK, :] = xf[:, cols]
        stack_own[q * TOK : (q + 1) * TOK, :] = xb[:, cols]
        stack_own[256 + q * TOK : 256 + (q + 1) * TOK, :] = cg[:, cols]
    own = meta[...]
    place(own[2:4], own[2:4], stack_own, w1)
    group = (core * 4 + py) * 4
    latent_at = pl.ds(pl.multiple_of((group + px) * TOK, 16), TOK)
    latent_got[latent_at, :] = latent[...]

    pl.semaphore_wait(barrier, 34)
    z_meta = to_zpeer(0, meta, meta_peer)
    z_xg = to_zpeer(1, stack_own, stack_peer)
    z_f = to_zpeer(2, stack_f.at[pl.ds(0, 256)], stack_f.at[pl.ds(256, 256)])
    z_cols = to_zpeer(3, cols_own, cols_peer)
    z_meta.start()
    z_xg.start()
    start1, recv1, sent1 = plane(0, w1, a1, SLOT, ex)
    start1()

    def latent_copy(i, at, device):
        return pltpu.make_async_remote_copy(
            src_ref=latent_got.at[at], dst_ref=latent_got.at[at], send_sem=l_send.at[i], recv_sem=l_recv.at[i],
            device_id=(pi, dp, device), device_id_type=MESH,
        )

    along_x = [latent_copy(i, latent_at, (py * 4 + lax.rem(px + 1 + i, 4)) * 2 + core) for i in range(3)]
    row_at = pl.ds(pl.multiple_of(group * TOK, 16), 4 * TOK)
    along_y = [latent_copy(3 + i, row_at, (lax.rem(py + 1 + i, 4) * 4 + px) * 2 + core) for i in range(3)]
    core_at = pl.ds(pl.multiple_of(core * 16 * TOK, 16), 16 * TOK)
    to_core = latent_copy(6, core_at, ex + 1 - 2 * core)
    for c in along_x:
        c.start()

    lane_e = lax.broadcasted_iota(jnp.int32, (TOK, EXPERTS), 1)

    def rates_of(tokens, names):
        logits = dot_nt(tokens[...], router[...])
        return [
            jax.nn.sigmoid(jnp.sum(jnp.where(lane_e == e.astype(jnp.int32), logits, 0.0), axis=1, keepdims=True)) for e in names
        ]

    rate_f = rates_of(xf, named[0:2])
    rate_b = rates_of(xb, named[2:4])
    total_f, total_b = rate_f[0] + rate_f[1], rate_b[0] + rate_b[1]
    gate_f = [ROUTE_SCALE * r / total_f for r in rate_f]
    gate_b = [ROUTE_SCALE * r / total_b for r in rate_b]
    cols_own[...] = columns(gate_f + gate_b + rate_b + [total_b])
    z_cols.start()

    for e in range(EXPERTS):
        halves = []
        for h in range(2):
            first = h * (D // 2) + e * KV_ROWS
            start = min(first // 128 * 128, D - 256)
            window = attn[:, start : start + 256].astype(F32)
            halves.append(pltpu.roll(window, (256 - (first - start) + h * 64) % 256, 1)[:, 0:128])
        attn_wire[e * TOK : (e + 1) * TOK, :] = jnp.where(lane < 64, halves[0], halves[1]).astype(BF)

    z_meta.wait_recv()
    peer = meta_peer[...]
    own_t, peer_t = own.T, peer.T

    def split(values):
        hi = values.astype(BF)
        return hi, (values - hi.astype(F32)).astype(BF)

    lane_w = lax.broadcasted_iota(jnp.int32, (TOK, WIRE), 1)

    def gate_rows(code0, code1, gate0, gate1, offset):
        value = jnp.where(lane_w == code0.astype(jnp.int32) + offset, gate0, 0.0)
        value = value + jnp.where(lane_w == code1.astype(jnp.int32) + offset, gate1, 0.0)
        return split(value)

    def forward_gates(j, m, gates):
        for q in range(Q):
            m_q = m[q * TOK : (q + 1) * TOK]
            hi, lo = gate_rows(m_q[:, 0:1], m_q[:, 1:2], gates[:, 0:1], gates[:, 1:2], j * CAP)
            g_pair[j * 512 + q * TOK : j * 512 + (q + 1) * TOK, :] = hi
            g_pair[j * 512 + 256 + q * TOK : j * 512 + 256 + (q + 1) * TOK, :] = lo

    forward_gates(0, own_t, cols_own[...])
    for q in range(S):
        m = own_t[0:TOK]
        hi, lo = gate_rows(m[:, 2:3], m[:, 3:4], cols_own[:, 2:3], cols_own[:, 3:4], q * CAP)
        g_part[q * TOK : (q + 1) * TOK, :] = hi
        g_part[S * TOK + q * TOK : S * TOK + (q + 1) * TOK, :] = lo
    for c in along_x:
        c.wait_recv()
    for c in along_y:
        c.start()

    z_xg.wait_recv()
    z_f.start()
    place(peer[2:4], peer[2:4], stack_peer, w2)
    start2, recv2, sent2 = plane(1, w2, a2, SLOT, ex)
    start2()

    def backward(rows_out, after=None):
        total = jnp.zeros((ROWS, 1), F32)
        for n in range(HALF // 256):
            cols = slice(n * 256, (n + 1) * 256)
            gate_act = dot(x2[0:ROWS, :], gate[:, cols])
            up_act = dot(x2[0:ROWS, :], up[:, cols])
            grad_hidden = dot_nt(x2[ROWS : 2 * ROWS, :], down[cols, :])
            sig = jax.nn.sigmoid(gate_act)
            active = gate_act * sig
            hidden = (active * up_act).astype(BF).astype(F32)
            total = total + jnp.sum(hidden * grad_hidden, axis=1, keepdims=True)
            gg[:, cols] = (grad_hidden * up_act * sig * (1.0 + gate_act * (1.0 - sig))).astype(BF)
            gu[:, cols] = (grad_hidden * active).astype(BF)
        for q in range(Q):
            cols = slice(q * PIECE, (q + 1) * PIECE)
            rows_out[:, cols] = (dot_nt(gg[...], gate[cols, :]) + dot_nt(gu[...], up[cols, :])).astype(BF)
            if after is not None:
                after[q].start()
        return total

    side = lax.broadcasted_iota(jnp.int32, (ROWS, 128), 1) < 64

    def hi_lo(total):
        hi, lo = split(total)
        return jnp.where(side, hi.astype(F32), lo.astype(F32)).astype(BF)

    for load in loads:
        load.wait()
    recv1()
    unpacked(a1)
    inner[0:ROWS, :] = hi_lo(backward(back_own))

    z_f.wait_recv()
    sent1()
    place(own[0:2], peer[0:2], stack_f, w1)
    start3, recv3, sent3 = plane(2, w1, a3, SLOT, ex)
    start3()
    for c in along_y:
        c.wait_recv()
    to_core.start()
    z_cols.wait_recv()
    forward_gates(1, peer_t, cols_peer[...])

    q_cols = [pl.ds(q * PIECE, PIECE) for q in range(Q)]
    z_back = [to_zpeer(4 + q, back_peer.at[:, q_cols[q]], back_got.at[:, q_cols[q]]) for q in range(Q)]
    z_inner = to_zpeer(8, inner.at[pl.ds(ROWS, ROWS)], inner_got)
    recv2()
    unpacked(a2)
    inner[ROWS : 2 * ROWS, :] = hi_lo(backward(back_peer, z_back))
    z_inner.start()

    recv3()
    start_a, recv_a, sent_a = plane(5, attn_wire, attn_got, TOK, group + px)
    start_a()
    unpacked(a3)
    for n in range(HALF // 256):
        cols = slice(n * 256, (n + 1) * 256)
        gate_act = dot(x2[...], gate[:, cols])
        up_act = dot(x2[...], up[:, cols])
        hid[:, cols] = (gate_act * jax.nn.sigmoid(gate_act) * up_act).astype(BF)
    for q in range(Q):
        rows = dot(hid[...], down[:, q * PIECE : (q + 1) * PIECE]).astype(BF)
        for j in range(2):
            for g in range(4):
                at = g * 384 + j * 192 + q * 48
                fwd_rows[at : at + 48, :] = rows[j * ROWS + g * 48 : j * ROWS + (g + 1) * 48]
    sent2()

    def pack_forward(g, c):
        rows = pl.ds(pl.multiple_of(g * 384, 16), 384)
        w2[rows, :] = dot(pack[...], fwd_rows[rows, :]).astype(BF)
        return c

    lax.fori_loop(0, 4, pack_forward, 0)
    start4, recv4, sent4 = plane(3, w2, a4, SLOT, ex)
    start4()

    to_core.wait_recv()
    recv_a()
    kv_sum[...] = lax.dot_general(attn_got[...], latent_got[...], (((0,), (0,)), ((), ())), preferred_element_type=F32)
    z_kv = to_zpeer(9, kv_sum.at[pl.ds(pl.multiple_of((1 - dp) * 64, 8), KV_ROWS)], kv_got)
    z_kv.start()

    z_inner.wait_recv()
    total = inner[0:ROWS, :].astype(F32) + inner_got[...].astype(F32)
    inner_sum[...] = hi_lo(total[:, 0:1] + total[:, 64:65])
    iv_wire[...] = dot(pack_inner[...], inner_sum[...]).astype(BF)
    start_i, recv_i, sent_i = plane(4, iv_wire, iv_got, 16, ex)
    start_i()
    for c in z_back:
        c.wait_recv()
    sent3()

    def pack_back(g, c):
        rows = pl.ds(pl.multiple_of(g * 48, 16), 48)
        for q in range(S):
            cols = slice(q * PART, (q + 1) * PART)
            part[q * 48 : (q + 1) * 48, :] = (back_own[rows, cols].astype(F32) + back_got[rows, cols].astype(F32)).astype(BF)
        w1[pl.ds(pl.multiple_of(g * 384, 16), 384), 0:PART] = dot(pack_part[...], part[...]).astype(BF)
        return c

    lax.fori_loop(0, 4, pack_back, 0)
    start5, recv5, sent5 = plane(6, w1, a5, SLOT, ex, cols=PART)
    start5()
    z_kv.wait_recv()
    kv_out[...] = kv_sum[pl.ds(pl.multiple_of(dp * 64, 8), KV_ROWS), :] + kv_got[...]

    recv4()
    got = dot(g_pair[512:1024, :], a4[...])
    peer_part[...] = (got[0:256] + got[256:512]).astype(BF)
    q_rows = [pl.ds(q * TOK, TOK) for q in range(Q)]
    z_part = [to_zpeer(10 + q, peer_part.at[q_rows[q]], peer_got.at[q_rows[q]]) for q in range(Q)]
    for c in z_part:
        c.start()
    got = dot(g_pair[0:512, :], a4[...])
    acc[...] = got[0:256] + got[256:512]
    for q in range(Q):
        rows = slice(q * TOK, (q + 1) * TOK)
        acc[rows, :] = acc[rows, :] + xf[:, q * PIECE : (q + 1) * PIECE].astype(F32)

    recv_i()
    lane_i = lax.broadcasted_iota(jnp.int32, (TOK, EXPERTS * 16), 1)
    picks = [jnp.where(lane_i == own_t[0:TOK, 4 + k : 5 + k].astype(jnp.int32), 1.0, 0.0).astype(BF) for k in range(TOP)]
    val = dot(jnp.concatenate(picks, axis=0), iv_got[...])
    inner0 = val[0:64, 0:1] + val[0:64, 64:65]
    inner1 = val[64:128, 0:1] + val[64:128, 64:65]
    rate0, rate1, rate_total = cols_own[:, 4:5], cols_own[:, 5:6], cols_own[:, 6:7]
    weighted = (inner0 * rate0 + inner1 * rate1) / (rate_total * rate_total)
    logit0 = ROUTE_SCALE * (inner0 / rate_total - weighted) * rate0 * (1.0 - rate0)
    logit1 = ROUTE_SCALE * (inner1 / rate_total - weighted) * rate1 * (1.0 - rate1)
    dlogits = jnp.where(lane_e == named[2].astype(jnp.int32), logit0, 0.0)
    dlogits = (dlogits + jnp.where(lane_e == named[3].astype(jnp.int32), logit1, 0.0)).astype(BF)
    rest = dot(dlogits, router[...]) + cg[...].astype(F32)

    def to_next(i, src, dst):
        return pltpu.make_async_remote_copy(
            src_ref=src, dst_ref=dst, send_sem=p_send.at[i], recv_sem=p_recv.at[i], device_id=ahead, device_id_type=MESH
        )

    n_y = [to_next(q, y_send.at[q_rows[q]], y_got.at[q_rows[q]]) for q in range(Q)]
    for q in range(Q):
        rows = slice(q * TOK, (q + 1) * TOK)
        z_part[q].wait_recv()
        y_send[rows, :] = (acc[rows, :] + peer_got[rows, :].astype(F32)).astype(BF)
        n_y[q].start()

    recv5()
    got = dot(g_part[...], a5[...])
    for q in range(S):
        cols = slice(q * PART, (q + 1) * PART)
        dx = rest[:, cols] + got[q * TOK : (q + 1) * TOK] + got[(S + q) * TOK : (S + q + 1) * TOK]
        dx_send[:, cols] = dx.astype(BF)
    n_dx = to_next(4, dx_send, dx_got)
    n_dx.start()

    for q in range(Q):
        n_y[q].wait_recv()
        fwd_out[:, q * PIECE : (q + 1) * PIECE] = y_got[q * TOK : (q + 1) * TOK, :]
    n_dx.wait_recv()
    bwd_out[...] = dx_got[...]

    for sent in (sent4, sent_i, sent5, sent_a):
        sent()
    for copy in [z_meta, z_f, z_xg, z_cols, z_inner, z_kv, n_dx, to_core] + z_back + z_part + n_y + along_x + along_y:
        copy.wait_send()


def body(x_fwd, routes_fwd, x_bwd, cot_bwd, routes_bwd, router_weight, gate_weight, up_weight, down_weight, attn_input, latent_cot):
    consts = [jnp.asarray(c, BF) for c in permutations()]
    vmem = pl.BlockSpec(memory_space=pltpu.VMEM)
    anywhere = pl.BlockSpec(memory_space=pl.ANY)
    V = pltpu.VMEM
    dma = pltpu.SemaphoreType.DMA
    scratch = [
        V((D, HALF), BF), V((D, HALF), BF), V((HALF, D), BF),
        V((512, PIECE), BF), V((512, PIECE), BF), V((512, PIECE), BF),
        V((8, Q * TOK), F32), V((8, Q * TOK), F32), V((TOK, 128), F32), V((TOK, 128), F32),
        V((WIRE, PIECE), BF), V((WIRE, PIECE), BF),
        V((WIRE, PIECE), BF), V((WIRE, PIECE), BF), V((WIRE, PIECE), BF),
        V((2 * ROWS, D), BF), V((ROWS, HALF), BF), V((ROWS, HALF), BF), V((2 * ROWS, HALF), BF),
        V((2 * ROWS, 128), BF), V((ROWS, 128), BF), V((ROWS, 128), BF),
        V((ROWS, D), BF), V((ROWS, D), BF), V((ROWS, D), BF),
        V((WIRE, PIECE), BF), V((WIRE, PIECE), BF),
        V((WIRE, PART), BF), V((S * 48, PART), BF),
        V((EXPERTS * 16, 128), BF), V((EXPERTS * 16, 128), BF),
        V((2 * S * TOK, WIRE), BF), V((1024, WIRE), BF),
        V((256, PIECE), F32), V((256, PIECE), BF), V((256, PIECE), BF),
        V((EXPERTS * TOK, 128), BF), V((EXPERTS * TOK, 128), BF), V((EXPERTS * TOK, LATENT), BF), V((128, LATENT), F32), V((KV_ROWS, LATENT), F32),
        V((256, PIECE), BF), V((TOK, D), BF), V((256, PIECE), BF), V((TOK, D), BF),
        dma((3,)), dma((14,)), dma((14,)), dma((7, 31)), dma((7, 31)), dma((7,)), dma((7,)), dma((7,)), dma((5,)), dma((5,)),
    ]
    fwd, bwd, kv = pl.pallas_call(
        kernel,
        out_shape=[
            jax.ShapeDtypeStruct((TOK, D), BF),
            jax.ShapeDtypeStruct((TOK, D), BF),
            jax.ShapeDtypeStruct((KV_ROWS, LATENT), F32),
        ],
        in_specs=[vmem] * 12 + [anywhere] * 3,
        out_specs=[vmem] * 3,
        scratch_shapes=scratch,
        compiler_params=pltpu.CompilerParams(collective_id=0, has_side_effects=True, vmem_limit_bytes=63 * 2**20),
        name="layer",
    )(
        x_fwd[0], x_bwd[0], cot_bwd[0], routes_fwd[0].T, routes_bwd[0].T, attn_input[0], latent_cot[0], router_weight[0].T, *consts,
        gate_weight[0, 0], up_weight[0, 0], down_weight[0, 0],
    )
    return fwd[None], bwd[None], kv[None]


def solution(mesh):
    tokens = P("pipe", ("dp", "expert"), None)
    in_specs = (
        tokens, tokens, tokens, tokens, tokens,
        P("pipe", None, None),
        P("pipe", "expert", None, "dp"),
        P("pipe", "expert", None, "dp"),
        P("pipe", "expert", "dp", None),
        tokens, tokens,
    )
    return jax.shard_map(body, mesh=mesh, in_specs=in_specs, out_specs=(tokens,) * 3, check_vma=False)
```

time: 274 us -> 243 us (0.89)
  the two profiles are of different devices: /device:TPU:176 before, /device:TPU:196 now
where the time goes in v2:
time: 243 us
  Pallas kernels  237 us (98%)
  local copies, waits for them, and re-layouts  5.18 us (2%)
    pallas_call x1, Pallas kernels, body(): pl.pallas_call(kernel, out_shape=[jax.ShapeDtypeStruct((TOK, D), BF), jax...  237 us
    unnamed x3, local copies, waits for them, and re-layouts  5.18 us

profile of v2, /device:TPU:196, one launch (start us, length us, event | category | flops | bytes accessed | tf_op | source)
XLA Modules:
  0.0 243.2 jit_solution(3712129117692113631)
XLA Ops:
  0.6 237.3 %layer.1 = (bf16[64,3584]{1,0:T(8,128)(2,1)}, bf16[64,3584]{1,0:T(8,128)(2,1)}, f32[56,512]{1,0:T(8,128)}) custom-call(bf16[64,3584]{1,0:T(8,128)(2,1)} %bitcast.25, bf16[64,3584]{1,0:T(8,128)(2,1)} %bitcast.26, bf16[64,3584]{1,0:T(8,128)(2,1)} %bitcast.27, s32[2,64]{1,0:T(2,128)} %bitcast.32, s32[2,64]{1,0:T(2,128)} %bitcast.33, bf16[64,3584]{1,0:T(8,128)(2,1)} %bitcast.28, ...), custom_call_target="tpu_custom_call" | custom-call | tf_op jit(solution)/shard_map/layer/pallas_call | solution.py:500
  238.0 1.8 copy.21
  239.8 1.8 copy.22
  241.6 1.6 copy.23

commit v3 on v2

--- a/solution.py
+++ b/solution.py
@@ -25,6 +25,7 @@
 ROWS = EXPERTS * CAP
 CHUNK = 8
 KV_ROWS = 56
+LANES = ((0, 512), (512, PIECE))
 MESH = pl.DeviceIdType.MESH
 BF = jnp.bfloat16
 F32 = jnp.float32
@@ -63,8 +64,8 @@
     xf, xb, cg, routes_f, routes_b, attn, latent, router, unpack, pack, pack_part, pack_inner,
     gate_hbm, up_hbm, down_hbm,
     fwd_out, bwd_out, kv_out,
-    gate, up, down, stack_f, stack_own, stack_peer, meta, meta_peer, cols_own, cols_peer,
-    w1, w2, a1, a2, a3, x2, gg, gu, hid, inner, inner_got, inner_sum,
+    gate, up, down, stack1, stack2, stack3, meta, meta_peer, cols_own, cols_peer,
+    w1, w2, a1, a2, a3, x2, x_own, gg, gu, hid, inner, inner_got, inner_sum,
     back_own, back_peer, back_got, fwd_rows, a4, a5, part,
     iv_wire, iv_got, g_part, g_pair, acc, peer_part, peer_got,
     attn_wire, attn_got, latent_got, kv_sum, kv_got, y_send, dx_send, y_got, dx_got,
@@ -96,16 +97,20 @@
     for load in loads:
         load.start()
 
-    def plane(unit, src, dst, rows, place_at, cols=None):
+    def plane(unit, src, dst, rows, place_at, lanes=None, land=None):
         def piece(e):
             at = pl.ds(pl.multiple_of(e * rows, 16), rows)
-            return src.at[at] if cols is None else src.at[at, pl.ds(0, cols)]
+            return src.at[at] if lanes is None else src.at[at, lanes]
+
+        landing = pl.ds(pl.multiple_of(place_at * rows, 16), rows)
+        landing = dst.at[landing] if land is None else dst.at[landing, land]
+        sample = dst.at[pl.ds(0, rows)] if land is None else dst.at[pl.ds(0, rows), land]
 
         def copy(i, dx, dy, dc):
             to = (lax.rem(py + dy, 4) * 4 + lax.rem(px + dx, 4)) * 2 + lax.rem(core + dc, 2)
             return pltpu.make_async_remote_copy(
                 src_ref=piece(to),
-                dst_ref=dst.at[pl.ds(pl.multiple_of(place_at * rows, 16), rows)],
+                dst_ref=landing,
                 send_sem=u_send.at[unit, i],
                 recv_sem=u_recv.at[unit, i],
                 device_id=(pi, dp, to),
@@ -115,7 +120,7 @@
         def local():
             return pltpu.make_async_copy(
                 piece(ex),
-                dst.at[pl.ds(pl.multiple_of(place_at * rows, 16), rows)],
+                landing,
                 local_sem.at[unit],
             )
 
@@ -133,7 +138,7 @@
 
         def wait_recv():
             def step(i, c):
-                pltpu.make_async_copy(dst.at[pl.ds(0, rows)], dst.at[pl.ds(0, rows)], u_recv.at[unit, i]).wait()
+                pltpu.make_async_copy(sample, sample, u_recv.at[unit, i]).wait()
                 return c
 
             lax.fori_loop(0, 31, step, 0)
@@ -141,7 +146,7 @@
 
         def wait_send():
             def step(i, c):
-                pltpu.make_async_copy(dst.at[pl.ds(0, rows)], dst.at[pl.ds(0, rows)], u_send.at[unit, i]).wait()
+                pltpu.make_async_copy(sample, sample, u_send.at[unit, i]).wait()
                 return c
 
             lax.fori_loop(0, 31, step, 0)
@@ -153,29 +158,30 @@
             src_ref=src, dst_ref=dst, send_sem=z_send.at[i], recv_sem=z_recv.at[i], device_id=zpeer, device_id_type=MESH
         )
 
-    def place(code_a, code_b, stack, wire):
+    def place(code_a, code_b, stack, wire, low=0, high=PIECE):
         first = jnp.concatenate([code_a[0:1], code_b[0:1] + float(CAP)], axis=1).astype(jnp.int32)
         second = jnp.concatenate([code_a[1:2], code_b[1:2] + float(CAP)], axis=1).astype(jnp.int32)
 
         def step(g, c):
             row = lax.broadcasted_iota(jnp.int32, (192, 512), 0) + g * 192
             member = jnp.where((row == first) | (row == second), 1.0, 0.0).astype(BF)
-            wire[pl.ds(pl.multiple_of(g * 192, 16), 192), :] = dot(member, stack[...]).astype(BF)
+            wire[pl.ds(pl.multiple_of(g * 192, 16), 192), low:high] = dot(member, stack[:, low:high]).astype(BF)
             return c
 
         lax.fori_loop(0, 8, step, 0)
 
-    def unpacked(wire):
+    def unpacked(wire, *targets):
         def step(c, carry):
             rows = dot(unpack[...], wire[pl.ds(pl.multiple_of(c * 384, 16), 384), :]).astype(BF)
+            at = pl.ds(pl.multiple_of(c * 48, 16), 48)
             for j in range(2):
                 for q in range(Q):
-                    x2[pl.ds(pl.multiple_of(j * ROWS + c * 48, 16), 48), q * PIECE : (q + 1) * PIECE] = rows[
-                        j * 192 + q * 48 : j * 192 + (q + 1) * 48
-                    ]
+                    targets[j][at, q * PIECE : (q + 1) * PIECE] = rows[j * 192 + q * 48 : j * 192 + (q + 1) * 48]
             return carry
 
         lax.fori_loop(0, 4, step, 0)
+
+    x_rows, g_rows = x2.at[pl.ds(0, ROWS)], x2.at[pl.ds(ROWS, ROWS)]
 
     lane = lax.broadcasted_iota(jnp.int32, (TOK, 128), 1)
 
@@ -209,22 +215,28 @@
 
     for q in range(Q):
         cols = slice(q * PIECE, (q + 1) * PIECE)
-        stack_f[q * TOK : (q + 1) * TOK, :] = xf[:, cols]
-        stack_own[q * TOK : (q + 1) * TOK, :] = xb[:, cols]
-        stack_own[256 + q * TOK : 256 + (q + 1) * TOK, :] = cg[:, cols]
+        stack1[q * TOK : (q + 1) * TOK, :] = xf[:, cols]
+        stack1[256 + q * TOK : 256 + (q + 1) * TOK, :] = xb[:, cols]
+        stack3[q * TOK : (q + 1) * TOK, :] = cg[:, cols]
     own = meta[...]
-    place(own[2:4], own[2:4], stack_own, w1)
+    place(own[0:2], own[2:4], stack1, w1)
     group = (core * 4 + py) * 4
     latent_at = pl.ds(pl.multiple_of((group + px) * TOK, 16), TOK)
     latent_got[latent_at, :] = latent[...]
 
     pl.semaphore_wait(barrier, 34)
     z_meta = to_zpeer(0, meta, meta_peer)
-    z_xg = to_zpeer(1, stack_own, stack_peer)
-    z_f = to_zpeer(2, stack_f.at[pl.ds(0, 256)], stack_f.at[pl.ds(256, 256)])
+    top, bottom = pl.ds(0, 256), pl.ds(256, 256)
+    z_xg = []
+    for i, (low, high) in enumerate(LANES):
+        lanes = pl.ds(low, high - low)
+        z_xg.append(to_zpeer(14 + 2 * i, stack1.at[bottom, lanes], stack2.at[top, lanes]))
+        z_xg.append(to_zpeer(15 + 2 * i, stack3.at[top, lanes], stack2.at[bottom, lanes]))
+    z_f = to_zpeer(2, stack1.at[top], stack3.at[bottom])
     z_cols = to_zpeer(3, cols_own, cols_peer)
     z_meta.start()
-    z_xg.start()
+    z_xg[0].start()
+    z_xg[1].start()
     start1, recv1, sent1 = plane(0, w1, a1, SLOT, ex)
     start1()
 
@@ -269,6 +281,16 @@
 
     z_meta.wait_recv()
     peer = meta_peer[...]
+    z_xg[0].wait_recv()
+    z_xg[1].wait_recv()
+    z_xg[2].start()
+    z_xg[3].start()
+    second = []
+    for unit, (low, high) in zip((1, 7), LANES):
+        lanes = pl.ds(low, high - low)
+        second.append(plane(unit, w2, a2, SLOT, ex, lanes, lanes))
+    place(peer[2:4], peer[2:4], stack2, w2, *LANES[0])
+    second[0][0]()
     own_t, peer_t = own.T, peer.T
 
     def split(values):
@@ -300,19 +322,19 @@
     for c in along_y:
         c.start()
 
-    z_xg.wait_recv()
+    z_xg[2].wait_recv()
+    z_xg[3].wait_recv()
     z_f.start()
-    place(peer[2:4], peer[2:4], stack_peer, w2)
-    start2, recv2, sent2 = plane(1, w2, a2, SLOT, ex)
-    start2()
-
-    def backward(rows_out, after=None):
+    place(peer[2:4], peer[2:4], stack2, w2, *LANES[1])
+    second[1][0]()
+
+    def backward(x, g, rows_out, after=None):
         total = jnp.zeros((ROWS, 1), F32)
         for n in range(HALF // 256):
             cols = slice(n * 256, (n + 1) * 256)
-            gate_act = dot(x2[0:ROWS, :], gate[:, cols])
-            up_act = dot(x2[0:ROWS, :], up[:, cols])
-            grad_hidden = dot_nt(x2[ROWS : 2 * ROWS, :], down[cols, :])
+            gate_act = dot(x[...], gate[:, cols])
+            up_act = dot(x[...], up[:, cols])
+            grad_hidden = dot_nt(g[...], down[cols, :])
             sig = jax.nn.sigmoid(gate_act)
             active = gate_act * sig
             hidden = (active * up_act).astype(BF).astype(F32)
@@ -332,15 +354,27 @@
         hi, lo = split(total)
         return jnp.where(side, hi.astype(F32), lo.astype(F32)).astype(BF)
 
+    def forward(j):
+        for n in range(HALF // 256):
+            cols = slice(n * 256, (n + 1) * 256)
+            gate_act = dot(x_rows[...], gate[:, cols])
+            up_act = dot(x_rows[...], up[:, cols])
+            hid[:, cols] = (gate_act * jax.nn.sigmoid(gate_act) * up_act).astype(BF)
+        for q in range(Q):
+            rows = dot(hid[...], down[:, q * PIECE : (q + 1) * PIECE]).astype(BF)
+            for g in range(4):
+                at = g * 384 + j * 192 + q * 48
+                fwd_rows[at : at + 48, :] = rows[g * 48 : (g + 1) * 48]
+
     for load in loads:
         load.wait()
     recv1()
-    unpacked(a1)
-    inner[0:ROWS, :] = hi_lo(backward(back_own))
+    unpacked(a1, x_rows, x_own)
+    forward(0)
 
     z_f.wait_recv()
     sent1()
-    place(own[0:2], peer[0:2], stack_f, w1)
+    place(own[2:4], peer[0:2], stack3, w1)
     start3, recv3, sent3 = plane(2, w1, a3, SLOT, ex)
     start3()
     for c in along_y:
@@ -352,27 +386,19 @@
     q_cols = [pl.ds(q * PIECE, PIECE) for q in range(Q)]
     z_back = [to_zpeer(4 + q, back_peer.at[:, q_cols[q]], back_got.at[:, q_cols[q]]) for q in range(Q)]
     z_inner = to_zpeer(8, inner.at[pl.ds(ROWS, ROWS)], inner_got)
-    recv2()
-    unpacked(a2)
-    inner[ROWS : 2 * ROWS, :] = hi_lo(backward(back_peer, z_back))
+    for unit in second:
+        unit[1]()
+    unpacked(a2, x_rows, g_rows)
+    inner[ROWS : 2 * ROWS, :] = hi_lo(backward(x_rows, g_rows, back_peer, z_back))
     z_inner.start()
 
     recv3()
     start_a, recv_a, sent_a = plane(5, attn_wire, attn_got, TOK, group + px)
     start_a()
-    unpacked(a3)
-    for n in range(HALF // 256):
-        cols = slice(n * 256, (n + 1) * 256)
-        gate_act = dot(x2[...], gate[:, cols])
-        up_act = dot(x2[...], up[:, cols])
-        hid[:, cols] = (gate_act * jax.nn.sigmoid(gate_act) * up_act).astype(BF)
-    for q in range(Q):
-        rows = dot(hid[...], down[:, q * PIECE : (q + 1) * PIECE]).astype(BF)
-        for j in range(2):
-            for g in range(4):
-                at = g * 384 + j * 192 + q * 48
-                fwd_rows[at : at + 48, :] = rows[j * ROWS + g * 48 : j * ROWS + (g + 1) * 48]
-    sent2()
+    unpacked(a3, g_rows, x_rows)
+    forward(1)
+    for unit in second:
+        unit[2]()
 
     def pack_forward(g, c):
         rows = pl.ds(pl.multiple_of(g * 384, 16), 384)
@@ -382,6 +408,8 @@
     lax.fori_loop(0, 4, pack_forward, 0)
     start4, recv4, sent4 = plane(3, w2, a4, SLOT, ex)
     start4()
+
+    inner[0:ROWS, :] = hi_lo(backward(x_own, g_rows, back_own))
 
     to_core.wait_recv()
     recv_a()
@@ -408,7 +436,7 @@
         return c
 
     lax.fori_loop(0, 4, pack_back, 0)
-    start5, recv5, sent5 = plane(6, w1, a5, SLOT, ex, cols=PART)
+    start5, recv5, sent5 = plane(6, w1, a5, SLOT, ex, pl.ds(0, PART))
     start5()
     z_kv.wait_recv()
     kv_out[...] = kv_sum[pl.ds(pl.multiple_of(dp * 64, 8), KV_ROWS), :] + kv_got[...]
@@ -469,8 +497,13 @@
 
     for sent in (sent4, sent_i, sent5, sent_a):
         sent()
-    for copy in [z_meta, z_f, z_xg, z_cols, z_inner, z_kv, n_dx, to_core] + z_back + z_part + n_y + along_x + along_y:
+    for copy in z_xg + [z_meta, z_f, z_cols, z_inner, z_kv, n_dx, to_core] + z_back + z_part + n_y + along_x + along_y:
         copy.wait_send()
+
+
+def handed_on(*refs):
+    for i in range(3):
+        refs[3 + i][...] = refs[i][...]
 
 
 def body(x_fwd, routes_fwd, x_bwd, cot_bwd, routes_bwd, router_weight, gate_weight, up_weight, down_weight, attn_input, latent_cot):
@@ -485,7 +518,7 @@
         V((8, Q * TOK), F32), V((8, Q * TOK), F32), V((TOK, 128), F32), V((TOK, 128), F32),
         V((WIRE, PIECE), BF), V((WIRE, PIECE), BF),
         V((WIRE, PIECE), BF), V((WIRE, PIECE), BF), V((WIRE, PIECE), BF),
-        V((2 * ROWS, D), BF), V((ROWS, HALF), BF), V((ROWS, HALF), BF), V((2 * ROWS, HALF), BF),
+        V((2 * ROWS, D), BF), V((ROWS, D), BF), V((ROWS, HALF), BF), V((ROWS, HALF), BF), V((ROWS, HALF), BF),
         V((2 * ROWS, 128), BF), V((ROWS, 128), BF), V((ROWS, 128), BF),
         V((ROWS, D), BF), V((ROWS, D), BF), V((ROWS, D), BF),
         V((WIRE, PIECE), BF), V((WIRE, PIECE), BF),
@@ -495,7 +528,7 @@
         V((256, PIECE), F32), V((256, PIECE), BF), V((256, PIECE), BF),
         V((EXPERTS * TOK, 128), BF), V((EXPERTS * TOK, 128), BF), V((EXPERTS * TOK, LATENT), BF), V((128, LATENT), F32), V((KV_ROWS, LATENT), F32),
         V((256, PIECE), BF), V((TOK, D), BF), V((256, PIECE), BF), V((TOK, D), BF),
-        dma((3,)), dma((14,)), dma((14,)), dma((7, 31)), dma((7, 31)), dma((7,)), dma((7,)), dma((7,)), dma((5,)), dma((5,)),
+        dma((3,)), dma((18,)), dma((18,)), dma((8, 31)), dma((8, 31)), dma((8,)), dma((7,)), dma((7,)), dma((5,)), dma((5,)),
     ]
     fwd, bwd, kv = pl.pallas_call(
         kernel,
@@ -513,6 +546,13 @@
         x_fwd[0], x_bwd[0], cot_bwd[0], routes_fwd[0].T, routes_bwd[0].T, attn_input[0], latent_cot[0], router_weight[0].T, *consts,
         gate_weight[0, 0], up_weight[0, 0], down_weight[0, 0],
     )
+    fwd, bwd, kv = pl.pallas_call(
+        handed_on,
+        out_shape=[jax.ShapeDtypeStruct(a.shape, a.dtype) for a in (fwd, bwd, kv)],
+        in_specs=[vmem] * 3,
+        out_specs=[vmem] * 3,
+        name="outputs",
+    )(fwd, bwd, kv)
     return fwd[None], bwd[None], kv[None]
 
 

time: 243 us -> 239 us (0.984)
  the two profiles are of different devices: /device:TPU:196 before, /device:TPU:72 now
where the time goes in v3:
time: 239 us
  Pallas kernels  239 us (100%)
    pallas_call x1, Pallas kernels, body(): pl.pallas_call(kernel, out_shape=[jax.ShapeDtypeStruct((TOK, D), BF), jax...  236 us

profile of v3, /device:TPU:72, one launch (start us, length us, event | category | flops | bytes accessed | tf_op | source)
XLA Modules:
  0.0 239.2 jit_solution(17286419153980681855)
XLA Ops:
  0.6 236.4 %layer.1 = (bf16[64,3584]{1,0:T(8,128)(2,1)}, bf16[64,3584]{1,0:T(8,128)(2,1)}, f32[56,512]{1,0:T(8,128)}) custom-call(bf16[64,3584]{1,0:T(8,128)(2,1)} %bitcast.23, bf16[64,3584]{1,0:T(8,128)(2,1)} %bitcast.24, bf16[64,3584]{1,0:T(8,128)(2,1)} %bitcast.25, s32[2,64]{1,0:T(2,128)} %bitcast.29, s32[2,64]{1,0:T(2,128)} %bitcast.30, bf16[64,3584]{1,0:T(8,128)(2,1)} %bitcast.26, ...), custom_call_target="tpu_custom_call" | custom-call | tf_op jit(solution)/shard_map/layer/pallas_call | solution.py:533
  237.0 2.2 outputs.1

commit v4 on v3

--- a/solution.py
+++ b/solution.py
@@ -125,14 +125,13 @@
             )
 
         def start():
-            def step(i, c):
+            def step(dc, i, c):
                 tx, ty = c
-                dx, dy = lax.rem(tx, 4), lax.rem(ty, 4)
-                copy(2 * i, dx, dy, 0).start()
-                copy(2 * i + 1, dx, dy, 1).start()
+                copy(15 * dc + i, lax.rem(tx, 4), lax.rem(ty, 4), dc).start()
                 return lax.div(tx, 4), lax.div(ty, 4)
 
-            lax.fori_loop(0, 15, step, (jnp.int32(STEPS_X), jnp.int32(STEPS_Y)))
+            for dc in range(2):
+                lax.fori_loop(0, 15, functools.partial(step, dc), (jnp.int32(STEPS_X), jnp.int32(STEPS_Y)))
             copy(30, 0, 0, 1).start()
             local().start()
 
@@ -473,13 +472,6 @@
             src_ref=src, dst_ref=dst, send_sem=p_send.at[i], recv_sem=p_recv.at[i], device_id=ahead, device_id_type=MESH
         )
 
-    n_y = [to_next(q, y_send.at[q_rows[q]], y_got.at[q_rows[q]]) for q in range(Q)]
-    for q in range(Q):
-        rows = slice(q * TOK, (q + 1) * TOK)
-        z_part[q].wait_recv()
-        y_send[rows, :] = (acc[rows, :] + peer_got[rows, :].astype(F32)).astype(BF)
-        n_y[q].start()
-
     recv5()
     got = dot(g_part[...], a5[...])
     for q in range(S):
@@ -488,6 +480,13 @@
         dx_send[:, cols] = dx.astype(BF)
     n_dx = to_next(4, dx_send, dx_got)
     n_dx.start()
+
+    n_y = [to_next(q, y_send.at[q_rows[q]], y_got.at[q_rows[q]]) for q in range(Q)]
+    for q in range(Q):
+        rows = slice(q * TOK, (q + 1) * TOK)
+        z_part[q].wait_recv()
+        y_send[rows, :] = (acc[rows, :] + peer_got[rows, :].astype(F32)).astype(BF)
+        n_y[q].start()
 
     for q in range(Q):
         n_y[q].wait_recv()

time: 239 us -> 221 us (0.925)
  the two profiles are of different devices: /device:TPU:72 before, /device:TPU:32 now
where the time goes in v4:
time: 221 us; the launch traced here: 218 us
  Pallas kernels  218 us (99%)
    pallas_call x1, Pallas kernels, body(): pl.pallas_call(kernel, out_shape=[jax.ShapeDtypeStruct((TOK, D), BF), jax...  216 us

profile of v4, /device:TPU:32, one launch (start us, length us, event | category | flops | bytes accessed | tf_op | source)
XLA Modules:
  0.0 218.5 jit_solution(1889285708764761315)
XLA Ops:
  0.6 215.7 %layer.1 = (bf16[64,3584]{1,0:T(8,128)(2,1)}, bf16[64,3584]{1,0:T(8,128)(2,1)}, f32[56,512]{1,0:T(8,128)}) custom-call(bf16[64,3584]{1,0:T(8,128)(2,1)} %bitcast.23, bf16[64,3584]{1,0:T(8,128)(2,1)} %bitcast.24, bf16[64,3584]{1,0:T(8,128)(2,1)} %bitcast.25, s32[2,64]{1,0:T(2,128)} %bitcast.29, s32[2,64]{1,0:T(2,128)} %bitcast.30, bf16[64,3584]{1,0:T(8,128)(2,1)} %bitcast.26, ...), custom_call_target="tpu_custom_call" | custom-call | tf_op jit(solution)/shard_map/layer/pallas_call | solution.py:532
  216.3 2.2 outputs.1
